TPU v7x, 256 devices: a whole 4x4x8 slice. The times are simulated.
256 devices in a mesh: real: 4 (over x), cell: 64 (over z, y, core).
Axes of the slice: x: 4, y: 4, z: 8, core: 2. Of those that a mesh axis runs over, the one named last changes fastest.
Arguments:
- initial: float32 [8, 128, 64, 128], P('real', 'cell'), may hold values from 0 to 2
- velocity: float32 [8, 3, 128, 64, 128], P('real', None, 'cell'), may hold values from -1 to 1
- dispersion: float32 [8, 3, 128, 64, 128], P('real', None, 'cell'), may hold values from 0.05 to 0.5
- bounds: int32 [128, 64], P('cell'), may hold values from 64 to 128
- basis: bfloat16 [256, 128, 64, 128], P(None, 'cell'), may hold values from -0.005859375 to 0.005859375
Outputs:
- mean_field: float32 [128, 64, 128], P('cell')
- spread_field: float32 [128, 64, 128], P('cell')
- coord_mean: float32 [256], replicated
- coord_cov: float32 [256, 256], replicated
All inputs are finite; a program needn't handle non-finite values.
Results may differ from a plain program's by a relative error of at most 0.012.
Values sent between devices are 32-bit elements; how exact they have to be, the bound alone decides.
No kernel may reach another device: no remote copies, remote signals or barrier semaphores. Data moves between devices by JAX's collectives and lax.ppermute only.
A program may use at most 64 MiB of HBM per device.

v0:
```python
import jax
import jax.numpy as jnp
from jax import lax
from jax.sharding import PartitionSpec as P

STEPS = 2


DT = 0.15


def with_halo(cells, sides, width):
    for axis, dim in sides:
        count = lax.axis_size(axis)
        ends = count - 1
        head = lax.slice_in_dim(cells, 0, width, axis=dim)
        tail = lax.slice_in_dim(cells, cells.shape[dim] - width, cells.shape[dim], axis=dim)
        cells = jnp.concatenate(
            [
                lax.ppermute(tail, axis, [(i, (i + 1) % count) for i in range(ends)]),
                cells,
                lax.ppermute(head, axis, [((i + 1) % count, i) for i in range(ends)]),
            ],
            axis=dim,
        )
    return cells


def combined_all(part, axis, combine):
    gathered = jax.tree.map(lambda a: lax.all_gather(a, axis), part)

    def take(source):
        return jax.tree.map(lambda a: lax.dynamic_index_in_dim(a, source, 0, False), gathered)

    return lax.fori_loop(
        1, lax.axis_size(axis), lambda source, state: combine(state, take(source)), take(0)
    )


def face_flux(left, right, vleft, vright, dleft, dright, aleft, aright):
    speed = 0.5 * (vleft + vright)
    spread = 0.5 * (dleft + dright)
    return (
        aleft
        * aright
        * (
            jnp.maximum(speed, 0.0) * left
            + jnp.minimum(speed, 0.0) * right
            - spread * (right - left)
        )
    )


def advance(conc, veloc, disper, active):
    flux_x = face_flux(
        conc[:, :-1],
        conc[:, 1:],
        veloc[:, 0, :-1],
        veloc[:, 0, 1:],
        disper[:, 0, :-1],
        disper[:, 0, 1:],
        active[:-1],
        active[1:],
    )
    inner = conc[:, 1:-1]
    vin = veloc[:, :, 1:-1]
    din = disper[:, :, 1:-1]
    ain = active[1:-1]
    flux_y = face_flux(
        inner[:, :, :-1],
        inner[:, :, 1:],
        vin[:, 1, :, :-1],
        vin[:, 1, :, 1:],
        din[:, 1, :, :-1],
        din[:, 1, :, 1:],
        ain[:, :-1],
        ain[:, 1:],
    )
    flux_z = face_flux(
        inner[..., :-1],
        inner[..., 1:],
        vin[:, 2, ..., :-1],
        vin[:, 2, ..., 1:],
        din[:, 2, ..., :-1],
        din[:, 2, ..., 1:],
        ain[..., :-1],
        ain[..., 1:],
    )
    div_y = jnp.pad(flux_y, ((0, 0), (0, 0), (0, 1), (0, 0))) - jnp.pad(
        flux_y, ((0, 0), (0, 0), (1, 0), (0, 0))
    )
    div_z = jnp.pad(flux_z, ((0, 0), (0, 0), (0, 0), (0, 1))) - jnp.pad(
        flux_z, ((0, 0), (0, 0), (0, 0), (1, 0))
    )
    div_x = flux_x[:, 1:] - flux_x[:, :-1]
    return ain * (inner - DT * (div_x + div_y + div_z))


def unpack(stacked, count):
    planes = stacked.shape[1:]
    veloc = stacked[: 3 * count].reshape((count, 3) + planes)
    disper = stacked[3 * count : 6 * count].reshape((count, 3) + planes)
    return (veloc, disper, stacked[6 * count])


def chan_merge(first, second):
    count_a, field_a, fsq_a, coord_a, csq_a = first
    count_b, field_b, fsq_b, coord_b, csq_b = second
    total = count_a + count_b
    weight = count_a * count_b / total
    delta_field = field_b - field_a
    delta_coord = coord_b - coord_a
    field_mean = field_a + delta_field * (count_b / total)
    field_sq = fsq_a + fsq_b + delta_field * delta_field * weight
    coord_mean = coord_a + delta_coord * (count_b / total)
    coord_sq = csq_a + csq_b + delta_coord[:, None] * delta_coord[None, :] * weight
    return (total, field_mean, field_sq, coord_mean, coord_sq)


def shards(initial, velocity, dispersion, bounds, basis):
    count, width, rows, depth_n = initial.shape
    depth = lax.broadcasted_iota(jnp.int32, (width, rows, depth_n), 2)
    active = (depth < bounds[:, :, None]).astype(jnp.float32)
    stacked = jnp.concatenate(
        [
            velocity.reshape((3 * count, width, rows, depth_n)),
            dispersion.reshape((3 * count, width, rows, depth_n)),
            active[None],
        ],
        axis=0,
    )
    start_conc = initial * active
    widened = with_halo(stacked, (("cell", 1),), 1)
    veloc, disper, act = unpack(widened, count)
    conc = start_conc
    for step in range(STEPS):
        padded = with_halo(conc, (("cell", 1),), 1)
        conc = advance(padded, veloc, disper, act)
    final = conc.astype(jnp.bfloat16)
    components = basis.shape[0]
    partial_coords = lax.dot_general(
        final.reshape(count, -1),
        basis.reshape(components, -1),
        (((1,), (1,)), ((), ())),
        preferred_element_type=jnp.float32,
    )
    coords = lax.psum(partial_coords, "cell")
    local_field = jnp.mean(conc, axis=0)
    local_fsq = jnp.sum((conc - local_field) ** 2, axis=0)
    local_coord = jnp.mean(coords, axis=0)
    centred = coords - local_coord
    local_csq = jnp.dot(
        centred.T, centred, precision=lax.Precision.HIGHEST, preferred_element_type=jnp.float32
    )
    number = jnp.array(count, jnp.float32)
    merged = combined_all(
        (number, local_field, local_fsq, local_coord, local_csq), "real", chan_merge
    )
    total_n, mean_field, field_sq, coord_mean, coord_sq = merged
    spread_field = field_sq / (total_n - 1.0)
    coord_cov = coord_sq / (total_n - 1.0)
    return (mean_field, spread_field, coord_mean, coord_cov)


def solution(mesh):
    placed = (
        P("real", "cell", None, None),
        P("real", None, "cell", None, None),
        P("real", None, "cell", None, None),
        P("cell", None),
        P(None, "cell", None, None),
    )
    return jax.shard_map(
        shards,
        mesh=mesh,
        in_specs=placed,
        out_specs=(P("cell", None, None), P("cell", None, None), P(), P()),
        check_vma=False,
    )
```

profile of v0, /device:TPU:128, one launch (start us, length us, event | category | flops | bytes accessed | tf_op | source)
XLA Modules:
  0.0 245.6 jit_solution(5680193027813562273)
XLA Ops:
  7.2 0.0 copy-start.1
  7.2 0.0 copy-start
  7.2 0.0 copy-start.3
  7.2 0.0 all-gather.7.cloned.1.call-start
  7.2 0.8 fusion.53
  8.1 1.2 pad_maximum_fusion
  9.3 0.0 slice-start
  9.3 0.1 fusion.59
  9.4 2.2 collective-permute-start
  11.5 7.0 %collective-permute-start.1 = (f32[13,1,64,128]{3,2,1,0:T(8,128)S(1)}, f32[13,1,64,128]{3,2,1,0:T(8,128)S(1)}, u32[]{:S(2)}, u32[]{:S(2)}) collective-permute-start(f32[13,1,64,128]{3,2,1,0:T(8,128)S(1)} %get-tuple-element.308), channel_id=1, source_target_pairs={{1,0},{2,1},{3,2},{4,3},{5,4},{6,5},{7,6},{8,7},{9,8},{10,9},{11,1... | collective-permute-start | bytes 1277960 | tf_op jit(solution)/shard_map/ppermute | solution.py:22
  18.5 0.8 fusion.52
  19.3 0.9 broadcast_multiply_fusion
  20.2 1.9 collective-permute-start.2
  22.2 7.0 %collective-permute-start.3 = (f32[2,1,64,128]{3,2,1,0:T(8,128)S(1)}, f32[2,1,64,128]{3,2,1,0:T(8,128)S(1)}, u32[]{:S(2)}, u32[]{:S(2)}) collective-permute-start(f32[2,1,64,128]{3,2,1,0:T(8,128)S(1)} %get-tuple-element.312), channel_id=1, source_target_pairs={{1,0},{2,1},{3,2},{4,3},{5,4},{6,5},{7,6},{8,7},{9,8},{10,9},{11,1... | collective-permute-start | bytes 196616 | tf_op jit(solution)/shard_map/ppermute | solution.py:22
  29.1 0.1 slice_multiply_fusion
  29.2 0.0 collective-permute-done
  29.2 0.0 collective-permute-done.1
  29.3 1.2 pad_maximum_fusion.1
  30.5 0.1 fusion.45
  30.6 0.2 fusion.39
  30.8 0.0 copy-done.1
  30.8 0.0 copy-done
  30.8 0.0 slice-start.1
  30.8 0.0 copy-start.5
  30.9 0.0 collective-permute-done.2
  30.9 0.1 collective-permute-done.3
  31.0 0.1 fusion.14
  31.1 0.0 copy-done.3
  31.1 0.1 fusion.36
  31.3 0.1 fusion.48
  31.3 2.1 collective-permute-start.4
  33.4 7.0 %collective-permute-start.5 = (f32[2,1,64,128]{3,2,1,0:T(8,128)S(1)}, f32[2,1,64,128]{3,2,1,0:T(8,128)S(1)}, u32[]{:S(2)}, u32[]{:S(2)}) collective-permute-start(f32[2,1,64,128]{3,2,1,0:T(8,128)S(1)} %get-tuple-element.310), channel_id=1, source_target_pairs={{1,0},{2,1},{3,2},{4,3},{5,4},{6,5},{7,6},{8,7},{9,8},{10,9},{11,1... | collective-permute-start | bytes 196616 | tf_op jit(solution)/shard_map/ppermute | solution.py:22
  40.4 0.2 fusion.42
  40.6 0.0 collective-permute-done.4
  40.6 1.7 collective-permute-done.5
  42.3 0.1 fusion.17
  42.4 0.1 fusion.57
  42.5 0.0 slice-done
  42.5 0.0 slice-done.1
  42.5 8.5 %fusion.4 = f32[2,256]{1,0:T(2,128)S(1)} fusion(bf16[256,2,64,128]{3,2,1,0:T(8,128)(2,1)S(1)} %bitcast.258, bf16[2,2,64,128]{3,2,1,0:T(8,128)(2,1)S(1)} %get-tuple-element.301), kind=kOutput, calls=%fused_computation.10 | convolution fusion | flops 16777216 | bytes 8456192 | tf_op jit(solution)/shard_map/dot_general | solution.py:141
  51.0 129.1 %psum.7 = f32[2,256]{1,0:T(2,128)S(1)} all-reduce(f32[2,256]{1,0:T(2,128)S(1)} %fusion.4), channel_id=1, replica_groups=mesh['real'=4,'cell'=64] {'cell'}, use_global_device_ids=true, to_apply=%region_2.3 | all-reduce | flops 512 | bytes 4096 | tf_op jit(solution)/shard_map/psum | solution.py:147
  180.2 1.1 fusion.54
  181.3 0.0 all-gather.7.cloned.1.call-update
  181.3 0.0 copy-done.5
  181.3 0.6 dynamic-slice
  181.9 0.8 dynamic-update-slice
  182.7 10.5 %all-reduce.8 = f32[4]{0:T(128)S(1)} all-reduce(f32[4]{0:T(128)S(1)} %dynamic-update-slice), channel_id=1, replica_groups=mesh['real'=4,'cell'=64] {'real'}, use_global_device_ids=true, to_apply=%add.8 | all-reduce | flops 4 | bytes 32
  193.2 7.0 %all-gather.4 = f32[4,1,256]{2,1,0:T(1,128)S(1)} all-gather(f32[1,1,256]{2,1,0:T(1,128)S(1)} %bitcast.271), channel_id=4, replica_groups=mesh['real'=4,'cell'=64] {'real'}, dimensions={0}, use_global_device_ids=true | all-gather | bytes 5120 | tf_op jit(solution)/shard_map/all_gather | solution.py:30
  200.2 12.6 %all-gather.1 = f32[8,64,128]{2,1,0:T(8,128)S(1)} all-gather(f32[2,64,128]{2,1,0:T(8,128)S(1)} %multiply_reduce_fusion), channel_id=3, replica_groups=mesh['real'=4,'cell'=64] {'real'}, dimensions={0}, use_global_device_ids=true | all-gather | bytes 327680 | tf_op jit(solution)/shard_map/all_gather | solution.py:30
  212.8 12.2 %all-gather = f32[8,64,128]{2,1,0:T(8,128)S(1)} all-gather(f32[2,64,128]{2,1,0:T(8,128)S(1)} %broadcast_multiply_fusion.1), channel_id=2, replica_groups=mesh['real'=4,'cell'=64] {'real'}, dimensions={0}, use_global_device_ids=true | all-gather | bytes 327680 | tf_op jit(solution)/shard_map/all_gather | solution.py:30
  225.0 0.0 all-gather.7.cloned.1.call-done
  225.1 1.0 slice.249
  226.0 11.3 %while.23 = (s32[]{:T(128)}, f32[]{:T(128)}, f32[2,64,128]{2,1,0:T(8,128)S(1)}, f32[2,64,128]{2,1,0:T(8,128)S(1)}, f32[256]{0:T(256)S(1)}, /*index=5*/f32[256,25...) while((s32[]{:T(128)}, f32[]{:T(128)}, ...), condition=%wide.region_5.6_spmd, body=%wide.region_4.5_spmd.sunk | while | flops 377609 | bytes 1188111 | solution.py:35
  226.1 0.6 dynamic_slice.91
  228.7 1.1 fusion.65
  229.8 0.6 dynamic_slice.91
  232.4 1.1 fusion.65
  233.6 0.6 dynamic_slice.91
  236.2 1.1 fusion.65
  237.4 0.0 copy-start.2
  237.4 0.0 copy-start.4
  237.4 0.7 broadcast_divide_fusion
  238.1 0.6 broadcast_divide_fusion.1
  238.8 0.0 copy-done.2
  (25 shorter events, 0.3 us)
Async XLA Ops:
  7.2 23.6 %copy-start.1 = (f32[2,3,2,64,128]{4,3,2,1,0:T(8,128)S(1)}, f32[2,3,2,64,128]{4,3,2,1,0:T(8,128)}, u32[]{:S(2)}) copy-start(f32[2,3,2,64,128]{4,3,2,1,0:T(8,128)} %param.8) | copy-start | bytes 1179652
  7.2 23.6 %copy-start = (f32[2,3,2,64,128]{4,3,2,1,0:T(8,128)S(1)}, f32[2,3,2,64,128]{4,3,2,1,0:T(8,128)}, u32[]{:S(2)}) copy-start(f32[2,3,2,64,128]{4,3,2,1,0:T(8,128)} %param.9) | copy-start | bytes 1179652
  7.2 23.9 %copy-start.3 = (f32[2,2,64,128]{3,2,1,0:T(8,128)S(1)}, f32[2,2,64,128]{3,2,1,0:T(8,128)}, u32[]{:S(2)}) copy-start(f32[2,2,64,128]{3,2,1,0:T(8,128)} %param.7) | copy-start | bytes 393220
  7.2 217.8 %all-gather.7.cloned.1.call-start = ((), (), s32[]{:S(2)}) async-start(), calls=%async_computation | async-start | bytes 1310720 | tf_op jit(solution)/shard_map/all_gather | solution.py:30
  9.3 33.2 %slice-start = ((s8[8388608]{0:T(1024)(128)(4,1)}), s8[4194304]{0:T(1024)(128)(4,1)S(1)}, s32[]{:S(2)}) async-start(s8[8388608]{0:T(1024)(128)(4,1)} %bitcast.257), calls=%async_computation.1 | async-start | bytes 8388608
  9.4 19.9 %collective-permute-start = (f32[13,1,64,128]{3,2,1,0:T(8,128)S(1)}, f32[13,1,64,128]{3,2,1,0:T(8,128)S(1)}, u32[]{:S(2)}, u32[]{:S(2)}) collective-permute-start(f32[13,1,64,128]{3,2,1,0:T(8,128)S(1)} %get-tuple-element.307), channel_id=1, source_target_pairs={{0,1},{1,2},{2,3},{3,4},{4,5},{5,6},{6,7},{7,8},{8,9},{9,10},{10,1... | collective-permute-start | bytes 1277960 | tf_op jit(solution)/shard_map/ppermute | solution.py:20
  11.5 17.7 %collective-permute-start.1 = (f32[13,1,64,128]{3,2,1,0:T(8,128)S(1)}, f32[13,1,64,128]{3,2,1,0:T(8,128)S(1)}, u32[]{:S(2)}, u32[]{:S(2)}) collective-permute-start(f32[13,1,64,128]{3,2,1,0:T(8,128)S(1)} %get-tuple-element.308), channel_id=1, source_target_pairs={{1,0},{2,1},{3,2},{4,3},{5,4},{6,5},{7,6},{8,7},{9,8},{10,9},{11,1... | collective-permute-start | bytes 1277960 | tf_op jit(solution)/shard_map/ppermute | solution.py:22
  20.2 10.6 %collective-permute-start.2 = (f32[2,1,64,128]{3,2,1,0:T(8,128)S(1)}, f32[2,1,64,128]{3,2,1,0:T(8,128)S(1)}, u32[]{:S(2)}, u32[]{:S(2)}) collective-permute-start(f32[2,1,64,128]{3,2,1,0:T(8,128)S(1)} %get-tuple-element.311), channel_id=1, source_target_pairs={{0,1},{1,2},{2,3},{3,4},{4,5},{5,6},{6,7},{7,8},{8,9},{9,10},{10,1... | collective-permute-start | bytes 196616 | tf_op jit(solution)/shard_map/ppermute | solution.py:20
  22.2 8.9 %collective-permute-start.3 = (f32[2,1,64,128]{3,2,1,0:T(8,128)S(1)}, f32[2,1,64,128]{3,2,1,0:T(8,128)S(1)}, u32[]{:S(2)}, u32[]{:S(2)}) collective-permute-start(f32[2,1,64,128]{3,2,1,0:T(8,128)S(1)} %get-tuple-element.312), channel_id=1, source_target_pairs={{1,0},{2,1},{3,2},{4,3},{5,4},{6,5},{7,6},{8,7},{9,8},{10,9},{11,1... | collective-permute-start | bytes 196616 | tf_op jit(solution)/shard_map/ppermute | solution.py:22
  30.8 11.7 %slice-start.1 = ((s8[8388608]{0:T(1024)(128)(4,1)}), s8[4194304]{0:T(1024)(128)(4,1)S(1)}, s32[]{:S(2)}) async-start(s8[8388608]{0:T(1024)(128)(4,1)} %bitcast.257), calls=%async_computation.2 | async-start | bytes 8388608
  30.8 150.5 %copy-start.5 = (u32[256]{0:T(256)S(1)}, u32[256]{0:T(256)}, u32[]{:S(2)}) copy-start(u32[256]{0:T(256)} %constant.109) | copy-start | bytes 3076
  31.3 9.2 %collective-permute-start.4 = (f32[2,1,64,128]{3,2,1,0:T(8,128)S(1)}, f32[2,1,64,128]{3,2,1,0:T(8,128)S(1)}, u32[]{:S(2)}, u32[]{:S(2)}) collective-permute-start(f32[2,1,64,128]{3,2,1,0:T(8,128)S(1)} %get-tuple-element.309), channel_id=1, source_target_pairs={{0,1},{1,2},{2,3},{3,4},{4,5},{5,6},{6,7},{7,8},{8,9},{9,10},{10,1... | collective-permute-start | bytes 196616 | tf_op jit(solution)/shard_map/ppermute | solution.py:20
  33.4 8.9 %collective-permute-start.5 = (f32[2,1,64,128]{3,2,1,0:T(8,128)S(1)}, f32[2,1,64,128]{3,2,1,0:T(8,128)S(1)}, u32[]{:S(2)}, u32[]{:S(2)}) collective-permute-start(f32[2,1,64,128]{3,2,1,0:T(8,128)S(1)} %get-tuple-element.310), channel_id=1, source_target_pairs={{1,0},{2,1},{3,2},{4,3},{5,4},{6,5},{7,6},{8,7},{9,8},{10,9},{11,1... | collective-permute-start | bytes 196616 | tf_op jit(solution)/shard_map/ppermute | solution.py:22
  237.4 1.4 copy-start.2
  237.4 1.4 copy-start.4
Sparse Core Ops, SparseCore 0:
  181.4 25.9 all-gather.6
where the time goes:
time: 246 us
  blocking collectives  171 us (70%)
  starting transfers between devices  27.1 us (11%)
  between operations  14.4 us (6%)
  other arithmetic  10.8 us (4%)
  matrix products  9.62 us (4%)
  loops' own time  6.13 us (2%)
  local copies, waits for them, and re-layouts  4.25 us (2%)
    psum x1, blocking collectives, shards(): coords = lax.psum(partial_coords, 'cell')  129 us
    all_gather x3, blocking collectives, combined_all(): gathered = jax.tree.map(lambda a: lax.all_gather(a, axis), part)  31.8 us
    ppermute x3, starting transfers between devices, with_halo(): lax.ppermute(head, axis, [((i + 1) % count, i) for i in range(ends)])  20.9 us
    unnamed x1, blocking collectives  10.5 us
    dot_general x1, matrix products, shards(): lax.dot_general(final.reshape(count, -1), basis.reshape(components, -1),...  8.48 us
    ppermute x3, starting transfers between devices, with_halo(): lax.ppermute(tail, axis, [(i, (i + 1) % count) for i in range(ends)])  6.16 us
    another operation x1, loops' own time, combined_all(): lax.fori_loop(1, lax.axis_size(axis), lambda source, state: combine(state...  6.13 us
  transfers between devices with their start and end apart: 7, of which 2 were waited for; matrix products, arithmetic and copies ran while one was open for 2% of the time, Pallas kernels for 0%

commit v1 on v0

v1 whole, which is shorter than its diff:
```python
import jax
import jax.numpy as jnp
from jax import lax
from jax.experimental import pallas as pl
from jax.experimental.pallas import tpu as pltpu
from jax.sharding import Mesh, PartitionSpec as P

DT = 0.15
CHUNKS = 8
PACK_LIMIT = 60
HOLD_LIMIT = 48
HOLD_MICROS = 10


def roll(a, shift, axis):
    return pltpu.roll(a, shift % a.shape[axis], axis)


def coefs(v, d, act, axis, last):
    speed = 0.5 * (v + roll(v, -1, axis))
    spread = 0.5 * (d + roll(d, -1, axis))
    both = jnp.where(last, 0.0, DT * act * roll(act, -1, axis))
    return both * (spread + jnp.maximum(speed, 0.0)), both * (spread - jnp.minimum(speed, 0.0))


def face(v_lo, v_hi, d_lo, d_hi, both):
    speed = 0.5 * (v_lo + v_hi)
    spread = 0.5 * (d_lo + d_hi)
    return both * (spread + jnp.maximum(speed, 0.0)), both * (spread - jnp.minimum(speed, 0.0))


def outflow(pq, c, axis):
    flux = pq[0] * c - pq[1] * roll(c, -1, axis)
    return flux - roll(flux, 1, axis)


def activity(bounds_ref, plane, rows, depth):
    limit = jnp.broadcast_to(bounds_ref[plane : plane + 1, :], (depth, rows))
    z = lax.broadcasted_iota(jnp.int32, (depth, rows), 0)
    return jnp.where(z < limit, 1.0, 0.0).astype(jnp.float32).T


def own_terms(r, init_ref, vel_ref, disp_ref, act, last_y, last_z):
    conc = [init_ref[r, x] * act[x] for x in range(2)]
    inner = face(
        vel_ref[r, 0, 0],
        vel_ref[r, 0, 1],
        disp_ref[r, 0, 0],
        disp_ref[r, 0, 1],
        DT * act[0] * act[1],
    )
    along = [
        (
            coefs(vel_ref[r, 1, x], disp_ref[r, 1, x], act[x], 0, last_y),
            coefs(vel_ref[r, 2, x], disp_ref[r, 2, x], act[x], 1, last_z),
        )
        for x in range(2)
    ]
    return conc, inner, along


def own_step(conc, inner, along):
    across = inner[0] * conc[0] - inner[1] * conc[1]
    return [
        conc[x]
        - (across if x == 0 else -across)
        - outflow(along[x][0], conc[x], 0)
        - outflow(along[x][1], conc[x], 1)
        for x in range(2)
    ]


def ends(rows, depth):
    last_y = lax.broadcasted_iota(jnp.int32, (rows, depth), 0) == rows - 1
    last_z = lax.broadcasted_iota(jnp.int32, (rows, depth), 1) == depth - 1
    return last_y, last_z


def fetch(copies):
    for copy in copies:
        copy.start()
    for copy in copies:
        copy.wait()


def pack_kernel(
    init_hbm, vel_hbm, disp_hbm, bounds_hbm, near_ref, far_ref,
    init_ref, vel_ref, disp_ref, bounds_ref, sems,
):
    count, _, rows, depth = init_ref.shape
    odd = lax.axis_index("core") == 1
    edge = lax.axis_index("chip") == jnp.where(odd, lax.axis_size("chip") - 1, 0)
    pairs = [(bounds_hbm, bounds_ref), (init_hbm, init_ref)]
    pairs += [(vel_hbm, vel_ref), (disp_hbm, disp_ref)]
    fetch([pltpu.make_async_copy(src, dst, sems.at[i]) for i, (src, dst) in enumerate(pairs)])
    act = [activity(bounds_ref, x, rows, depth) for x in range(2)]
    last_y, last_z = ends(rows, depth)
    for r in range(count):
        conc, inner, along = own_terms(r, init_ref, vel_ref, disp_ref, act, last_y, last_z)
        nxt = own_step(conc, inner, along)
        planes = [
            (nxt[x], conc[x], vel_ref[r, 0, x], disp_ref[r, 0, x] * act[x]) for x in range(2)
        ]
        for i in range(4):
            near_ref[4 * r + i] = jnp.where(odd, planes[0][i], planes[1][i])
            sent = jnp.where(odd, planes[1][i], planes[0][i])
            far_ref[4 * r + i] = jnp.where(edge, 0.0, sent) if i == 3 else sent


NEXT, CONC, VELX, DISPX, ALONG_Y, ALONG_Z, INNER, PLANES = 0, 2, 4, 6, 8, 12, 16, 18


def hold_kernel(
    after_ref, init_hbm, vel_hbm, disp_hbm, bounds_hbm, kept_ref,
    init_ref, vel_ref, disp_ref, bounds_ref, sems,
):
    count, _, rows, depth = init_ref.shape
    pairs = [(bounds_hbm, bounds_ref), (init_hbm, init_ref)]
    pairs += [(vel_hbm, vel_ref), (disp_hbm, disp_ref)]
    fetch([pltpu.make_async_copy(src, dst, sems.at[i]) for i, (src, dst) in enumerate(pairs)])
    act = [activity(bounds_ref, x, rows, depth) for x in range(2)]
    last_y, last_z = ends(rows, depth)
    for r in range(count):
        conc, inner, along = own_terms(r, init_ref, vel_ref, disp_ref, act, last_y, last_z)
        nxt = own_step(conc, inner, along)
        for x in range(2):
            kept_ref[r, NEXT + x] = nxt[x]
            kept_ref[r, CONC + x] = conc[x]
            kept_ref[r, VELX + x] = vel_ref[r, 0, x]
            kept_ref[r, DISPX + x] = disp_ref[r, 0, x] * act[x]
            for i in range(2):
                kept_ref[r, ALONG_Y + 2 * x + i] = along[x][0][i]
                kept_ref[r, ALONG_Z + 2 * x + i] = along[x][1][i]
        for i in range(2):
            kept_ref[r, INNER + i] = inner[i]


def step_kernel(
    kept_ref, near_ref, far_ref, held_ref, conc_ref, mine_ref, other_ref, part_ref
):
    count, _, rows, depth = kept_ref.shape
    components = held_ref.shape[0]
    chunk = components // CHUNKS
    odd = lax.axis_index("core") == 1
    weights = []
    for r in range(count):
        near = [near_ref[4 * r + i] for i in range(4)]
        far = [far_ref[4 * r + i] for i in range(4)]
        low = [jnp.where(odd, near[i], far[i]) for i in range(4)]
        high = [jnp.where(odd, far[i], near[i]) for i in range(4)]
        conc = [kept_ref[r, CONC + x] for x in range(2)]
        vx = [kept_ref[r, VELX + x] for x in range(2)]
        dx = [kept_ref[r, DISPX + x] for x in range(2)]
        both_lo = jnp.where((low[3] > 0.0) & (dx[0] > 0.0), DT, 0.0)
        both_hi = jnp.where((high[3] > 0.0) & (dx[1] > 0.0), DT, 0.0)
        lo_p, lo_q = face(low[2], vx[0], low[3], dx[0], both_lo)
        hi_p, hi_q = face(vx[1], high[2], dx[1], high[3], both_hi)
        flux_lo = lo_p * low[1] - lo_q * conc[0]
        flux_hi = hi_p * conc[1] - hi_q * high[1]
        below = low[0] - flux_lo
        above = high[0] + flux_hi
        conc = [kept_ref[r, NEXT] + flux_lo, kept_ref[r, NEXT + 1] - flux_hi]
        along = [
            [
                [kept_ref[r, base + 2 * x + i] for i in range(2)]
                for base in (ALONG_Y, ALONG_Z)
            ]
            for x in range(2)
        ]
        nxt = own_step(conc, [kept_ref[r, INNER + i] for i in range(2)], along)
        nxt[0] = nxt[0] + (lo_p * below - lo_q * conc[0])
        nxt[1] = nxt[1] - (hi_p * conc[1] - hi_q * above)
        for x in range(2):
            conc_ref[r, x] = nxt[x]
        weights.append(jnp.concatenate([nxt[0], nxt[1]], axis=1))
    weights = jnp.concatenate(weights, axis=0).T.astype(jnp.bfloat16)
    lane = lax.broadcasted_iota(jnp.int32, (8, count * rows), 1)
    group = (lane % rows) // 8
    for i in range(CHUNKS):
        b = held_ref[pl.ds(i * chunk, chunk)]
        b = jnp.concatenate(
            [b[:, 0].reshape(chunk * rows, depth), b[:, 1].reshape(chunk * rows, depth)], axis=1
        )
        every = jnp.dot(b, weights, preferred_element_type=jnp.float32)
        every = every.reshape(chunk, rows // 8, 8, count * rows)
        kept = every[:, 0]
        for j in range(1, rows // 8):
            kept = jnp.where((group == j)[None], every[:, j], kept)
        part_ref[pl.ds(i * chunk * 8, chunk * 8)] = kept.reshape(chunk * 8, count * rows)
    lane = lax.broadcasted_iota(jnp.int32, (components, count * rows), 1)
    diag = part_ref[pl.ds(0, components, stride=8)]
    for s in range(1, 8):
        diag = jnp.where(lane % 8 == s, part_ref[pl.ds(s, components, stride=8)], diag)
    pick = (
        lax.broadcasted_iota(jnp.int32, (8, count * rows), 1) // rows
        == lax.broadcasted_iota(jnp.int32, (8, count * rows), 0)
    ).astype(jnp.float32)
    coords = lax.dot_general(
        pick,
        diag,
        (((1,), (1,)), ((), ())),
        precision=lax.Precision.HIGHEST,
        preferred_element_type=jnp.float32,
    )
    half = components // 2
    for r in range(count):
        low, high = coords[r : r + 1, :half], coords[r : r + 1, half:]
        mine_ref[:, r * half : (r + 1) * half] = jnp.where(odd, high, low)
        other_ref[:, r * half : (r + 1) * half] = jnp.where(odd, low, high)


def cov_kernel(mine_ref, other_ref, mean_ref, cov_ref):
    odd = lax.axis_index("core") == 1
    mine, other = mine_ref[...], other_ref[...]
    coords = jnp.concatenate(
        [jnp.where(odd, other, mine), jnp.where(odd, mine, other)], axis=1
    )
    number = coords.shape[0]
    mean = jnp.sum(coords, axis=0, keepdims=True) * (1.0 / number)
    mean_ref[...] = mean
    centred = coords - mean
    cov_ref[...] = lax.dot_general(
        centred,
        centred,
        (((0,), (0,)), ((), ())),
        precision=lax.Precision.HIGHEST,
        preferred_element_type=jnp.float32,
    ) * (1.0 / (number - 1))


def tree_sum(terms):
    while len(terms) > 1:
        terms = [a + b for a, b in zip(terms[::2], terms[1::2])]
    return terms[0]


def stats_kernel(*refs):
    fields, (mean_ref, spread_ref) = refs[:-2], refs[-2:]
    values = [f[r] for f in fields for r in range(f.shape[0])]
    mean = tree_sum(values) * (1.0 / len(values))
    mean_ref[...] = mean
    spread_ref[...] = tree_sum([(v - mean) ** 2 for v in values]) * (1.0 / (len(values) - 1))


def call(kernel, out_shape, specs, scratch=(), limit=16, micros=0):
    return pl.pallas_call(
        kernel,
        out_shape=out_shape,
        in_specs=[pl.BlockSpec(memory_space=s) for s in specs],
        out_specs=jax.tree.map(lambda _: pl.BlockSpec(memory_space=pltpu.VMEM), out_shape),
        scratch_shapes=list(scratch),
        compiler_params=pltpu.CompilerParams(vmem_limit_bytes=int(limit * 2**20)),
        cost_estimate=pl.CostEstimate(
            flops=micros * 10**9, bytes_accessed=micros * 3 * 10**6, transcendentals=0
        )
        if micros
        else None,
    )


def shards(initial, velocity, dispersion, bounds, basis):
    count, width, rows, depth = initial.shape
    components = basis.shape[0]
    half = components // 2
    reals, chips, _ = (lax.axis_size(a) for a in ("real", "chip", "core"))
    f32 = jnp.float32
    vmem = pltpu.VMEM

    hbm = pltpu.HBM
    plane = (rows, depth)
    packed = jax.ShapeDtypeStruct((4 * count, rows, depth), f32)
    inputs = (initial, velocity, dispersion, bounds)
    own = [pltpu.VMEM(a.shape, a.dtype) for a in inputs] + [pltpu.SemaphoreType.DMA((4,))]
    near, far = call(pack_kernel, (packed, packed), [hbm] * 4, own, PACK_LIMIT)(*inputs)
    kept = call(
        hold_kernel,
        jax.ShapeDtypeStruct((count, PLANES, *plane), f32),
        [pl.ANY] + [hbm] * 4,
        own,
        HOLD_LIMIT,
        HOLD_MICROS,
    )(near, *inputs)
    cells = 2 * chips
    far = lax.ppermute(
        far,
        ("chip", "core"),
        [(i, ((i + 1) ^ 1) - 1 if 0 < i < cells - 1 else cells - 1 - i) for i in range(cells)],
    )
    near = lax.ppermute(near, "core", [(0, 1), (1, 0)])
    line = jax.ShapeDtypeStruct((1, count * half), f32)
    conc, mine, other = call(
        step_kernel,
        (jax.ShapeDtypeStruct(initial.shape, f32), line, line),
        [vmem] * 4,
        [pltpu.VMEM((components * 8, count * rows), f32)],
    )(kept, near, far, basis)

    mine = mine + lax.ppermute(other, "core", [(0, 1), (1, 0)])
    spots = reals * chips
    sent = jnp.broadcast_to(mine.reshape(1, 1, count * half), (spots, 1, count * half))
    got = lax.all_to_all(sent, ("real", "chip"), 0, 0, tiled=True)
    mine = got.reshape(reals, chips, count, half).sum(axis=1).reshape(reals * count, half)
    other = lax.ppermute(mine, "core", [(0, 1), (1, 0)])
    coord_mean, coord_cov = call(
        cov_kernel,
        (
            jax.ShapeDtypeStruct((1, components), f32),
            jax.ShapeDtypeStruct((components, components), f32),
        ),
        [vmem] * 2,
    )(mine, other)

    fields = [conc] + [
        lax.ppermute(conc, "real", [(i, i ^ k) for i in range(reals)])
        for k in range(1, reals)
    ]
    field = jax.ShapeDtypeStruct((width, rows, depth), f32)
    mean_field, spread_field = call(stats_kernel, (field, field), [vmem] * reals)(*fields)
    return mean_field, spread_field, coord_mean.reshape(components), coord_cov


def solution(mesh):
    reals, cells = mesh.devices.shape
    split = Mesh(mesh.devices.reshape(reals, cells // 2, 2), ("real", "chip", "core"))
    cell = ("chip", "core")
    return jax.shard_map(
        shards,
        mesh=split,
        in_specs=(
            P("real", cell, None, None),
            P("real", None, cell, None, None),
            P("real", None, cell, None, None),
            P(cell, None),
            P(None, cell, None, None),
        ),
        out_specs=(P(cell, None, None), P(cell, None, None), P(), P()),
        check_vma=False,
    )
```

time: 246 us -> 47.7 us (0.19)
  the two profiles are of different devices: /device:TPU:128 before, /device:TPU:1 now
where the time goes in v1:
time: 47.7 us; the launch traced here: 47.4 us
  starting transfers between devices  24.7 us (52%)
  waiting for transfers between devices  8.51 us (18%)
  Pallas kernels  8.14 us (17%)
  local copies, waits for them, and re-layouts  5.26 us (11%)
  between operations  0.71 us (1%)
    all_to_all x1, starting transfers between devices, shards(): got = lax.all_to_all(sent, ('real', 'chip'), 0, 0, tiled=True)  9.16 us
    all_to_all x1, waiting for transfers between devices, shards(): got = lax.all_to_all(sent, ('real', 'chip'), 0, 0, tiled=True)  7.6 us
    ppermute x1, starting transfers between devices, shards(): near = lax.ppermute(near, 'core', [(0, 1), (1, 0)])  6.56 us
    unnamed x14, local copies, waits for them, and re-layouts  4.53 us
    ppermute x3, starting transfers between devices, shards(): lax.ppermute(conc, 'real', [(i, i ^ k) for i in range(reals)])  3.34 us
    pallas_call x1, Pallas kernels, shards(): call(step_kernel, (jax.ShapeDtypeStruct(initial.shape, f32), line, line),...  3.01 us
    ppermute x1, starting transfers between devices, shards(): lax.ppermute(far, ('chip', 'core'), [(i, (i + 1 ^ 1) - 1 if 0 < i < cells...  2.77 us
    pallas_call x1, Pallas kernels, shards(): call(pack_kernel, (packed, packed), [hbm] * 4, own, PACK_LIMIT)(*inputs)  2.34 us
  transfers between devices with their start and end apart: 8, of which 3 were waited for; matrix products, arithmetic and copies ran while one was open for 0% of the time, Pallas kernels for 3%

profile of v1, /device:TPU:1, one launch (start us, length us, event | category | flops | bytes accessed | tf_op | source)
XLA Modules:
  0.0 47.4 jit_solution(15077941161089523116)
XLA Ops:
  0.6 2.3 %shard_map.84 = (f32[8,64,128]{2,1,0:T(8,128)}, f32[8,64,128]{2,1,0:T(8,128)}) custom-call(f32[2,2,64,128]{3,2,1,0:T(8,128)} %init_hbm.3, f32[2,3,2,64,128]{4,3,2,1,0:T(8,128)} %vel_hbm.3, f32[2,3,2,64,128]{4,3,2,1,0:T(8,128)} %disp_hbm.3, s32[2,64]{1,0:T(2,128)} %bounds_hbm.3), custom_call_target="tpu_custom_call" | custom-call | tf_op jit(solution)/shard_map/pallas_call | solution.py:274
  3.0 2.8 %collective-permute-start.1 = (f32[8,64,128]{2,1,0:T(8,128)}, f32[8,64,128]{2,1,0:T(8,128)S(1)}, u32[]{:S(2)}, u32[]{:S(2)}) collective-permute-start(f32[8,64,128]{2,1,0:T(8,128)} %get-tuple-element.14), channel_id=1, source_target_pairs={{0,63},{1,2},{2,1},{3,4},{4,3},{5,6},{6,5},{7,8},{8,7},{9,10},{10,... | collective-permute-start | bytes 786440 | tf_op jit(solution)/shard_map/ppermute | solution.py:284
  5.8 0.0 slice-start
  5.8 0.0 slice-start.1
  5.8 6.6 %collective-permute-start = (f32[8,64,128]{2,1,0:T(8,128)}, f32[8,64,128]{2,1,0:T(8,128)S(1)}, u32[]{:S(2)}, u32[]{:S(2)}) collective-permute-start(f32[8,64,128]{2,1,0:T(8,128)} %get-tuple-element.13.after_ref), channel_id=1, source_target_pairs={{0,1},{1,0},{2,3},{3,2},{4,5},{5,4},{6,7},{7,6},{8,9},{9,8},{10,11... | collective-permute-start | bytes 786440 | tf_op jit(solution)/shard_map/ppermute | solution.py:289
  12.3 0.0 copy-start
  12.3 1.0 %copy-done = f32[2,3,2,64,128]{4,3,2,1,0:T(8,128)S(1)} copy-done((f32[2,3,2,64,128]{4,3,2,1,0:T(8,128)S(1)}, f32[2,3,2,64,128]{4,3,2,1,0:T(8,128)}, u32[]{:S(2)}) %copy-start) | copy-done | bytes 393240
  13.3 0.0 copy-start.1
  13.3 1.0 %copy-done.1 = f32[2,3,2,64,128]{4,3,2,1,0:T(8,128)S(1)} copy-done((f32[2,3,2,64,128]{4,3,2,1,0:T(8,128)S(1)}, f32[2,3,2,64,128]{4,3,2,1,0:T(8,128)}, u32[]{:S(2)}) %copy-start.1) | copy-done | bytes 393240
  14.3 0.0 copy-start.2
  14.3 0.9 %copy-done.2 = f32[2,2,64,128]{3,2,1,0:T(8,128)S(1)} copy-done((f32[2,2,64,128]{3,2,1,0:T(8,128)S(1)}, f32[2,2,64,128]{3,2,1,0:T(8,128)}, u32[]{:S(2)}) %copy-start.2) | copy-done | bytes 131096
  15.2 0.0 copy-start.3
  15.2 0.7 %copy-done.3 = s32[2,64]{1,0:T(2,128)S(1)} copy-done((s32[2,64]{1,0:T(2,128)S(1)}, s32[2,64]{1,0:T(2,128)}, u32[]{:S(2)}) %copy-start.3) | copy-done | bytes 536
  15.9 0.0 copy-start.4
  15.9 0.9 %copy-done.4 = f32[8,64,128]{2,1,0:T(8,128)S(1)} copy-done((f32[8,64,128]{2,1,0:T(8,128)S(1)}, f32[8,64,128]{2,1,0:T(8,128)}, u32[]{:S(2)}) %copy-start.4) | copy-done | bytes 262168
  16.9 0.9 %shard_map.85.kept_ref = f32[2,18,64,128]{3,2,1,0:T(8,128)S(1)} custom-call(f32[8,64,128]{2,1,0:T(8,128)S(1)} %copy-done.4, f32[2,2,64,128]{3,2,1,0:T(8,128)S(1)} %copy-done.2, f32[2,3,2,64,128]{4,3,2,1,0:T(8,128)S(1)} %copy-done, f32[2,3,2,64,128]{4,3,2,1,0:T(8,128)S(1)} %copy-done.1, s32[2,64]{1,0:T(2,128)S(1)} %copy-done.3), custom_call_target="tpu_custom_call" | custom-call | flops 10000000000 | bytes 30000000 | tf_op jit(solution)/shard_map/pallas_call | solution.py:275
  17.8 0.0 collective-permute-done.1.far_ref
  17.8 0.0 collective-permute-done.near_ref
  17.8 0.0 slice-done
  17.8 0.0 slice-done.1
  17.8 3.0 %shard_map.86 = (f32[2,2,64,128]{3,2,1,0:T(8,128)S(1)}, f32[1,256]{1,0:T(1,128)S(1)}, f32[1,256]{1,0:T(1,128)S(1)}) custom-call(f32[2,18,64,128]{3,2,1,0:T(8,128)S(1)} %shard_map.85.kept_ref, f32[8,64,128]{2,1,0:T(8,128)S(1)} %collective-permute-done.near_ref, f32[8,64,128]{2,1,0:T(8,128)S(1)} %collective-permute-done.1.far_ref, ...), custom_call_target="tpu_custom_call" | custom-call | tf_op jit(solution)/shard_map/pallas_call | solution.py:291
  20.8 0.7 %collective-permute-start.5 = (f32[1,256]{1,0:T(1,128)S(1)}, f32[1,256]{1,0:T(1,128)S(1)}, u32[]{:S(2)}, u32[]{:S(2)}) collective-permute-start(f32[1,256]{1,0:T(1,128)S(1)} %get-tuple-element.19), channel_id=1, source_target_pairs={{0,1},{1,0},{2,3},{3,2},{4,5},{5,4},{6,7},{7,6},{8,9},{9,8},{10,11... | collective-permute-start | bytes 3080 | tf_op jit(solution)/shard_map/ppermute | solution.py:298
  21.6 0.8 %collective-permute-done.5 = f32[1,256]{1,0:T(1,128)S(1)} collective-permute-done((f32[1,256]{1,0:T(1,128)S(1)}, f32[1,256]{1,0:T(1,128)S(1)}, u32[]{:S(2)}, u32[]{:S(2)}) %collective-permute-start.5) | collective-permute-done | bytes 1056 | tf_op jit(solution)/shard_map/ppermute | solution.py:298
  22.4 0.7 %broadcast_in_dim.8 = f32[128,1,256]{2,1,0:T(1,128)} broadcast(f32[256]{0:T(256)S(1)} %bitcast.9), dimensions={2} | broadcast | bytes 132096 | tf_op jit(solution)/shard_map/broadcast_in_dim | solution.py:300
  23.1 9.2 %all-to-all-start = ((f32[128,1,256]{2,1,0:T(1,128)}), f32[128,1,256]{2,1,0:T(1,128)S(1)}, u32[]{:S(2)}, u32[]{:S(2)}) async-start(f32[128,1,256]{2,1,0:T(1,128)} %broadcast_in_dim.8), calls=%async_computation | async-start | bytes 262144 | tf_op jit(solution)/shard_map/all_to_all | solution.py:301
  32.3 2.4 %collective-permute-start.4 = (f32[2,2,64,128]{3,2,1,0:T(8,128)S(1)}, f32[2,2,64,128]{3,2,1,0:T(8,128)S(1)}, u32[]{:S(2)}, u32[]{:S(2)}) collective-permute-start(f32[2,2,64,128]{3,2,1,0:T(8,128)S(1)} %get-tuple-element.15.refs_0_), channel_id=1, source_target_pairs={{0,192},{64,128},{128,64},{192,0},{1,193},{65,129},{129,65},{193,1... | collective-permute-start | bytes 393224 | tf_op jit(solution)/shard_map/ppermute | solution.py:314
  34.7 0.2 collective-permute-start.3
  34.9 0.8 %collective-permute-start.2 = (f32[2,2,64,128]{3,2,1,0:T(8,128)S(1)}, f32[2,2,64,128]{3,2,1,0:T(8,128)S(1)}, u32[]{:S(2)}, u32[]{:S(2)}) collective-permute-start(f32[2,2,64,128]{3,2,1,0:T(8,128)S(1)} %get-tuple-element.15.refs_0_), channel_id=1, source_target_pairs={{0,64},{64,0},{128,192},{192,128},{1,65},{65,1},{129,193},{193,129... | collective-permute-start | bytes 393224 | tf_op jit(solution)/shard_map/ppermute | solution.py:314
  35.6 7.6 %all-to-all-done = f32[128,1,256]{2,1,0:T(1,128)S(1)} async-done(((f32[128,1,256]{2,1,0:T(1,128)}), f32[128,1,256]{2,1,0:T(1,128)S(1)}, u32[]{:S(2)}, u32[]{:S(2)}) %all-to-all-start) | async-done | bytes 131104 | tf_op jit(solution)/shard_map/all_to_all | solution.py:301
  43.3 2.2 %collective-permute-start.6 = (f32[8,128]{1,0:T(8,128)S(1)}, f32[8,128]{1,0:T(8,128)S(1)}, u32[]{:S(2)}, u32[]{:S(2)}) collective-permute-start(f32[8,128]{1,0:T(8,128)S(1)} %bitcast.6), channel_id=1, source_target_pairs={{0,1},{1,0},{2,3},{3,2},{4,5},{5,4},{6,7},{7,6},{8,9},{9,8},{10,11... | collective-permute-start | bytes 12296 | tf_op jit(solution)/shard_map/ppermute | solution.py:303
  45.5 0.0 collective-permute-done.4.refs_3_
  45.5 0.0 collective-permute-done.3.refs_2_
  45.5 0.0 collective-permute-done.2.refs_1_
  45.5 0.7 %shard_map.87 = (f32[2,64,128]{2,1,0:T(8,128)}, f32[2,64,128]{2,1,0:T(8,128)}) custom-call(f32[2,2,64,128]{3,2,1,0:T(8,128)S(1)} %get-tuple-element.15.refs_0_, f32[2,2,64,128]{3,2,1,0:T(8,128)S(1)} %collective-permute-done.2.refs_1_, f32[2,2,64,128]{3,2,1,0:T(8,128)S(1)} %collective-permute-done.3.refs_2_, f32[2,2,64,128]{3,2,1,0:T(8,128)S(1)} %collective-permute-done.4.refs_3_), custom_call_target="tpu_custom_call" | custom-call | tf_op jit(solution)/shard_map/pallas_call | solution.py:318
  46.2 0.1 collective-permute-done.6.other_ref
  46.3 1.1 %shard_map.88 = (f32[1,256]{1,0:T(1,128)}, f32[256,256]{1,0:T(8,128)}) custom-call(f32[8,128]{1,0:T(8,128)S(1)} %bitcast.7, f32[8,128]{1,0:T(8,128)S(1)} %collective-permute-done.6.other_ref), custom_call_target="tpu_custom_call" | custom-call | tf_op jit(solution)/shard_map/pallas_call | solution.py:304
  (3 shorter events, 0.0 us)
Async XLA Ops:
  3.0 14.8 %collective-permute-start.1 = (f32[8,64,128]{2,1,0:T(8,128)}, f32[8,64,128]{2,1,0:T(8,128)S(1)}, u32[]{:S(2)}, u32[]{:S(2)}) collective-permute-start(f32[8,64,128]{2,1,0:T(8,128)} %get-tuple-element.14), channel_id=1, source_target_pairs={{0,63},{1,2},{2,1},{3,4},{4,3},{5,6},{6,5},{7,8},{8,7},{9,10},{10,... | collective-permute-start | bytes 786440 | tf_op jit(solution)/shard_map/ppermute | solution.py:284
  5.8 12.0 %slice-start = ((s8[8388608]{0:T(1024)(128)(4,1)}), s8[4194304]{0:T(1024)(128)(4,1)S(1)}, s32[]{:S(2)}) async-start(s8[8388608]{0:T(1024)(128)(4,1)} %bitcast.4), calls=%async_computation.1 | async-start | bytes 8388608
  5.8 12.1 %slice-start.1 = ((s8[8388608]{0:T(1024)(128)(4,1)}), s8[4194304]{0:T(1024)(128)(4,1)S(1)}, s32[]{:S(2)}) async-start(s8[8388608]{0:T(1024)(128)(4,1)} %bitcast.4), calls=%async_computation.2 | async-start | bytes 8388608
  5.8 12.0 %collective-permute-start = (f32[8,64,128]{2,1,0:T(8,128)}, f32[8,64,128]{2,1,0:T(8,128)S(1)}, u32[]{:S(2)}, u32[]{:S(2)}) collective-permute-start(f32[8,64,128]{2,1,0:T(8,128)} %get-tuple-element.13.after_ref), channel_id=1, source_target_pairs={{0,1},{1,0},{2,3},{3,2},{4,5},{5,4},{6,7},{7,6},{8,9},{9,8},{10,11... | collective-permute-start | bytes 786440 | tf_op jit(solution)/shard_map/ppermute | solution.py:289
  12.3 1.0 %copy-start = (f32[2,3,2,64,128]{4,3,2,1,0:T(8,128)S(1)}, f32[2,3,2,64,128]{4,3,2,1,0:T(8,128)}, u32[]{:S(2)}) copy-start(f32[2,3,2,64,128]{4,3,2,1,0:T(8,128)} %vel_hbm.3) | copy-start | bytes 1179652
  13.3 1.0 %copy-start.1 = (f32[2,3,2,64,128]{4,3,2,1,0:T(8,128)S(1)}, f32[2,3,2,64,128]{4,3,2,1,0:T(8,128)}, u32[]{:S(2)}) copy-start(f32[2,3,2,64,128]{4,3,2,1,0:T(8,128)} %disp_hbm.3) | copy-start | bytes 1179652
  14.3 0.9 %copy-start.2 = (f32[2,2,64,128]{3,2,1,0:T(8,128)S(1)}, f32[2,2,64,128]{3,2,1,0:T(8,128)}, u32[]{:S(2)}) copy-start(f32[2,2,64,128]{3,2,1,0:T(8,128)} %init_hbm.3) | copy-start | bytes 393220
  15.2 0.7 %copy-start.3 = (s32[2,64]{1,0:T(2,128)S(1)}, s32[2,64]{1,0:T(2,128)}, u32[]{:S(2)}) copy-start(s32[2,64]{1,0:T(2,128)} %bounds_hbm.3) | copy-start | bytes 1540
  15.9 0.9 %copy-start.4 = (f32[8,64,128]{2,1,0:T(8,128)S(1)}, f32[8,64,128]{2,1,0:T(8,128)}, u32[]{:S(2)}) copy-start(f32[8,64,128]{2,1,0:T(8,128)} %get-tuple-element.13.after_ref) | copy-start | bytes 786436
  20.8 1.5 %collective-permute-start.5 = (f32[1,256]{1,0:T(1,128)S(1)}, f32[1,256]{1,0:T(1,128)S(1)}, u32[]{:S(2)}, u32[]{:S(2)}) collective-permute-start(f32[1,256]{1,0:T(1,128)S(1)} %get-tuple-element.19), channel_id=1, source_target_pairs={{0,1},{1,0},{2,3},{3,2},{4,5},{5,4},{6,7},{7,6},{8,9},{9,8},{10,11... | collective-permute-start | bytes 3080 | tf_op jit(solution)/shard_map/ppermute | solution.py:298
  23.1 20.1 %all-to-all-start = ((f32[128,1,256]{2,1,0:T(1,128)}), f32[128,1,256]{2,1,0:T(1,128)S(1)}, u32[]{:S(2)}, u32[]{:S(2)}) async-start(f32[128,1,256]{2,1,0:T(1,128)} %broadcast_in_dim.8), calls=%async_computation | async-start | bytes 262144 | tf_op jit(solution)/shard_map/all_to_all | solution.py:301
  32.3 13.2 %collective-permute-start.4 = (f32[2,2,64,128]{3,2,1,0:T(8,128)S(1)}, f32[2,2,64,128]{3,2,1,0:T(8,128)S(1)}, u32[]{:S(2)}, u32[]{:S(2)}) collective-permute-start(f32[2,2,64,128]{3,2,1,0:T(8,128)S(1)} %get-tuple-element.15.refs_0_), channel_id=1, source_target_pairs={{0,192},{64,128},{128,64},{192,0},{1,193},{65,129},{129,65},{193,1... | collective-permute-start | bytes 393224 | tf_op jit(solution)/shard_map/ppermute | solution.py:314
  34.7 10.8 %collective-permute-start.3 = (f32[2,2,64,128]{3,2,1,0:T(8,128)S(1)}, f32[2,2,64,128]{3,2,1,0:T(8,128)S(1)}, u32[]{:S(2)}, u32[]{:S(2)}) collective-permute-start(f32[2,2,64,128]{3,2,1,0:T(8,128)S(1)} %get-tuple-element.15.refs_0_), channel_id=1, source_target_pairs={{0,128},{64,192},{128,0},{192,64},{1,129},{65,193},{129,1},{193,65... | collective-permute-start | bytes 393224 | tf_op jit(solution)/shard_map/ppermute | solution.py:314
  34.9 10.6 %collective-permute-start.2 = (f32[2,2,64,128]{3,2,1,0:T(8,128)S(1)}, f32[2,2,64,128]{3,2,1,0:T(8,128)S(1)}, u32[]{:S(2)}, u32[]{:S(2)}) collective-permute-start(f32[2,2,64,128]{3,2,1,0:T(8,128)S(1)} %get-tuple-element.15.refs_0_), channel_id=1, source_target_pairs={{0,64},{64,0},{128,192},{192,128},{1,65},{65,1},{129,193},{193,129... | collective-permute-start | bytes 393224 | tf_op jit(solution)/shard_map/ppermute | solution.py:314
  43.3 3.0 %collective-permute-start.6 = (f32[8,128]{1,0:T(8,128)S(1)}, f32[8,128]{1,0:T(8,128)S(1)}, u32[]{:S(2)}, u32[]{:S(2)}) collective-permute-start(f32[8,128]{1,0:T(8,128)S(1)} %bitcast.6), channel_id=1, source_target_pairs={{0,1},{1,0},{2,3},{3,2},{4,5},{5,4},{6,7},{7,6},{8,9},{9,8},{10,11... | collective-permute-start | bytes 12296 | tf_op jit(solution)/shard_map/ppermute | solution.py:303

commit v2 on v1

--- a/solution.py
+++ b/solution.py
@@ -84,18 +84,31 @@
 
 
 def pack_kernel(
-    init_hbm, vel_hbm, disp_hbm, bounds_hbm, near_ref, far_ref,
-    init_ref, vel_ref, disp_ref, bounds_ref, sems,
+    init_hbm, vel_hbm, disp_hbm, bounds_hbm, near_hbm, far_hbm,
+    init_ref, vel_ref, disp_ref, bounds_ref, near_ref, far_ref, bounds_sem, sems, out_sems,
 ):
     count, _, rows, depth = init_ref.shape
     odd = lax.axis_index("core") == 1
     edge = lax.axis_index("chip") == jnp.where(odd, lax.axis_size("chip") - 1, 0)
-    pairs = [(bounds_hbm, bounds_ref), (init_hbm, init_ref)]
-    pairs += [(vel_hbm, vel_ref), (disp_hbm, disp_ref)]
-    fetch([pltpu.make_async_copy(src, dst, sems.at[i]) for i, (src, dst) in enumerate(pairs)])
+    limits = pltpu.make_async_copy(bounds_hbm, bounds_ref, bounds_sem)
+    limits.start()
+    fields = ((init_hbm, init_ref), (vel_hbm, vel_ref), (disp_hbm, disp_ref))
+    arrive = [
+        [
+            pltpu.make_async_copy(src.at[r], dst.at[r], sems.at[r, i])
+            for i, (src, dst) in enumerate(fields)
+        ]
+        for r in range(count)
+    ]
+    for copy in sum(arrive, []):
+        copy.start()
+    limits.wait()
     act = [activity(bounds_ref, x, rows, depth) for x in range(2)]
     last_y, last_z = ends(rows, depth)
+    leave = []
     for r in range(count):
+        for copy in arrive[r]:
+            copy.wait()
         conc, inner, along = own_terms(r, init_ref, vel_ref, disp_ref, act, last_y, last_z)
         nxt = own_step(conc, inner, along)
         planes = [
@@ -105,6 +118,12 @@
             near_ref[4 * r + i] = jnp.where(odd, planes[0][i], planes[1][i])
             sent = jnp.where(odd, planes[1][i], planes[0][i])
             far_ref[4 * r + i] = jnp.where(edge, 0.0, sent) if i == 3 else sent
+        part = pl.ds(4 * r, 4)
+        for i, (src, dst) in enumerate(((far_ref, far_hbm), (near_ref, near_hbm))):
+            leave.append(pltpu.make_async_copy(src.at[part], dst.at[part], out_sems.at[r, i]))
+            leave[-1].start()
+    for copy in leave:
+        copy.wait()
 
 
 NEXT, CONC, VELX, DISPX, ALONG_Y, ALONG_Z, INNER, PLANES = 0, 2, 4, 6, 8, 12, 16, 18
@@ -209,7 +228,16 @@
         other_ref[:, r * half : (r + 1) * half] = jnp.where(odd, low, high)
 
 
-def cov_kernel(mine_ref, other_ref, mean_ref, cov_ref):
+def tree_sum(terms):
+    while len(terms) > 1:
+        terms = [a + b for a, b in zip(terms[::2], terms[1::2])]
+    return terms[0]
+
+
+def stats_kernel(mine_ref, other_ref, *refs):
+    fields, refs = refs[:-9], refs[-9:]
+    (mean_hbm, spread_hbm, coord_hbm, cov_hbm), refs = refs[:4], refs[4:]
+    mean_ref, spread_ref, coord_ref, cov_ref, sems = refs
     odd = lax.axis_index("core") == 1
     mine, other = mine_ref[...], other_ref[...]
     coords = jnp.concatenate(
@@ -217,7 +245,7 @@
     )
     number = coords.shape[0]
     mean = jnp.sum(coords, axis=0, keepdims=True) * (1.0 / number)
-    mean_ref[...] = mean
+    coord_ref[...] = mean
     centred = coords - mean
     cov_ref[...] = lax.dot_general(
         centred,
@@ -226,28 +254,30 @@
         precision=lax.Precision.HIGHEST,
         preferred_element_type=jnp.float32,
     ) * (1.0 / (number - 1))
-
-
-def tree_sum(terms):
-    while len(terms) > 1:
-        terms = [a + b for a, b in zip(terms[::2], terms[1::2])]
-    return terms[0]
-
-
-def stats_kernel(*refs):
-    fields, (mean_ref, spread_ref) = refs[:-2], refs[-2:]
+    copies = [
+        pltpu.make_async_copy(cov_ref, cov_hbm, sems.at[0]),
+        pltpu.make_async_copy(coord_ref, coord_hbm, sems.at[1]),
+        pltpu.make_async_copy(mean_ref, mean_hbm, sems.at[2]),
+        pltpu.make_async_copy(spread_ref, spread_hbm, sems.at[3]),
+    ]
+    copies[0].start()
+    copies[1].start()
     values = [f[r] for f in fields for r in range(f.shape[0])]
     mean = tree_sum(values) * (1.0 / len(values))
     mean_ref[...] = mean
+    copies[2].start()
     spread_ref[...] = tree_sum([(v - mean) ** 2 for v in values]) * (1.0 / (len(values) - 1))
-
-
-def call(kernel, out_shape, specs, scratch=(), limit=16, micros=0):
+    copies[3].start()
+    for copy in copies:
+        copy.wait()
+
+
+def call(kernel, out_shape, specs, scratch=(), limit=16, micros=0, out=pltpu.VMEM):
     return pl.pallas_call(
         kernel,
         out_shape=out_shape,
         in_specs=[pl.BlockSpec(memory_space=s) for s in specs],
-        out_specs=jax.tree.map(lambda _: pl.BlockSpec(memory_space=pltpu.VMEM), out_shape),
+        out_specs=jax.tree.map(lambda _: pl.BlockSpec(memory_space=out), out_shape),
         scratch_shapes=list(scratch),
         compiler_params=pltpu.CompilerParams(vmem_limit_bytes=int(limit * 2**20)),
         cost_estimate=pl.CostEstimate(
@@ -270,13 +300,23 @@
     plane = (rows, depth)
     packed = jax.ShapeDtypeStruct((4 * count, rows, depth), f32)
     inputs = (initial, velocity, dispersion, bounds)
-    own = [pltpu.VMEM(a.shape, a.dtype) for a in inputs] + [pltpu.SemaphoreType.DMA((4,))]
-    near, far = call(pack_kernel, (packed, packed), [hbm] * 4, own, PACK_LIMIT)(*inputs)
+    own = [pltpu.VMEM(a.shape, a.dtype) for a in inputs]
+    dma = pltpu.SemaphoreType.DMA
+    near, far = call(
+        pack_kernel,
+        (packed, packed),
+        [hbm] * 4,
+        own
+        + [pltpu.VMEM(packed.shape, f32)] * 2
+        + [dma(()), dma((count, 3)), dma((count, 2))],
+        PACK_LIMIT,
+        out=hbm,
+    )(*inputs)
     kept = call(
         hold_kernel,
         jax.ShapeDtypeStruct((count, PLANES, *plane), f32),
         [pl.ANY] + [hbm] * 4,
-        own,
+        own + [dma((4,))],
         HOLD_LIMIT,
         HOLD_MICROS,
     )(near, *inputs)
@@ -301,21 +341,17 @@
     got = lax.all_to_all(sent, ("real", "chip"), 0, 0, tiled=True)
     mine = got.reshape(reals, chips, count, half).sum(axis=1).reshape(reals * count, half)
     other = lax.ppermute(mine, "core", [(0, 1), (1, 0)])
-    coord_mean, coord_cov = call(
-        cov_kernel,
-        (
-            jax.ShapeDtypeStruct((1, components), f32),
-            jax.ShapeDtypeStruct((components, components), f32),
-        ),
-        [vmem] * 2,
-    )(mine, other)
-
     fields = [conc] + [
-        lax.ppermute(conc, "real", [(i, i ^ k) for i in range(reals)])
-        for k in range(1, reals)
-    ]
-    field = jax.ShapeDtypeStruct((width, rows, depth), f32)
-    mean_field, spread_field = call(stats_kernel, (field, field), [vmem] * reals)(*fields)
+        lax.ppermute(conc, "real", [(i, i ^ k) for i in range(reals)]) for k in range(1, reals)
+    ]
+    shapes = ((width, rows, depth), (width, rows, depth), (1, components), (components, components))
+    mean_field, spread_field, coord_mean, coord_cov = call(
+        stats_kernel,
+        tuple(jax.ShapeDtypeStruct(a, f32) for a in shapes),
+        [vmem] * (2 + reals),
+        [pltpu.VMEM(a, f32) for a in shapes] + [dma((4,))],
+        out=hbm,
+    )(mine, other, *fields)
     return mean_field, spread_field, coord_mean.reshape(components), coord_cov
 
 

time: 47.7 us -> 47.7 us (level)
  waiting for transfers between devices: 8.51 us -> 9.24 us
  Pallas kernels: 8.14 us -> 7.44 us
    ppermute x1, waiting for transfers between devices: 0.08 us -> 0.81 us  [shards(): other = lax.ppermute(mine, 'core', [(0, 1), (1, 0)])]
    pallas_call x3 -> x2, Pallas kernels: 4.21 us -> 3.51 us  [the longest x1 2.28 us: shards(): call(pack_kernel, (packed, packed), [hbm] * 4, own + [pltpu.VMEM(packed.s...]
  transfers between devices with their start and end apart: 8 -> 8, of which waited for: 3 -> 3; matrix products, arithmetic and copies ran while one was open for 0% -> 0% of each run, Pallas kernels for 3% -> 2%
where the time goes in v2:
time: 47.7 us; the launch traced here: 47.4 us
  starting transfers between devices  24.7 us (52%)
  waiting for transfers between devices  9.24 us (19%)
  Pallas kernels  7.44 us (16%)
  local copies, waits for them, and re-layouts  5.26 us (11%)
  between operations  0.71 us (1%)
    all_to_all x1, starting transfers between devices, shards(): got = lax.all_to_all(sent, ('real', 'chip'), 0, 0, tiled=True)  9.16 us
    all_to_all x1, waiting for transfers between devices, shards(): got = lax.all_to_all(sent, ('real', 'chip'), 0, 0, tiled=True)  7.6 us
    ppermute x1, starting transfers between devices, shards(): near = lax.ppermute(near, 'core', [(0, 1), (1, 0)])  6.56 us
    unnamed x14, local copies, waits for them, and re-layouts  4.53 us
    ppermute x3, starting transfers between devices, shards(): lax.ppermute(conc, 'real', [(i, i ^ k) for i in range(reals)])  3.34 us
    pallas_call x1, Pallas kernels, shards(): call(step_kernel, (jax.ShapeDtypeStruct(initial.shape, f32), line, line),...  3.01 us
    ppermute x1, starting transfers between devices, shards(): lax.ppermute(far, ('chip', 'core'), [(i, (i + 1 ^ 1) - 1 if 0 < i < cells...  2.77 us
    pallas_call x1, Pallas kernels, shards(): call(pack_kernel, (packed, packed), [hbm] * 4, own + [pltpu.VMEM(packed.s...  2.28 us
  transfers between devices with their start and end apart: 8, of which 3 were waited for; matrix products, arithmetic and copies ran while one was open for 0% of the time, Pallas kernels for 2%

profile of v2, /device:TPU:1, one launch (start us, length us, event | category | flops | bytes accessed | tf_op | source)
XLA Modules:
  0.0 47.4 jit_solution(1061873484414929869)
XLA Ops:
  0.6 2.3 %shard_map.84 = (f32[8,64,128]{2,1,0:T(8,128)}, f32[8,64,128]{2,1,0:T(8,128)}) custom-call(f32[2,2,64,128]{3,2,1,0:T(8,128)} %init_hbm.3, f32[2,3,2,64,128]{4,3,2,1,0:T(8,128)} %vel_hbm.3, f32[2,3,2,64,128]{4,3,2,1,0:T(8,128)} %disp_hbm.3, s32[2,64]{1,0:T(2,128)} %bounds_hbm.3), custom_call_target="tpu_custom_call" | custom-call | tf_op jit(solution)/shard_map/pallas_call | solution.py:305
  2.9 2.8 %collective-permute-start.1 = (f32[8,64,128]{2,1,0:T(8,128)}, f32[8,64,128]{2,1,0:T(8,128)S(1)}, u32[]{:S(2)}, u32[]{:S(2)}) collective-permute-start(f32[8,64,128]{2,1,0:T(8,128)} %get-tuple-element.14), channel_id=1, source_target_pairs={{0,63},{1,2},{2,1},{3,4},{4,3},{5,6},{6,5},{7,8},{8,7},{9,10},{10,... | collective-permute-start | bytes 786440 | tf_op jit(solution)/shard_map/ppermute | solution.py:324
  5.7 0.0 slice-start
  5.7 0.0 slice-start.1
  5.7 6.6 %collective-permute-start = (f32[8,64,128]{2,1,0:T(8,128)}, f32[8,64,128]{2,1,0:T(8,128)S(1)}, u32[]{:S(2)}, u32[]{:S(2)}) collective-permute-start(f32[8,64,128]{2,1,0:T(8,128)} %get-tuple-element.13.after_ref), channel_id=1, source_target_pairs={{0,1},{1,0},{2,3},{3,2},{4,5},{5,4},{6,7},{7,6},{8,9},{9,8},{10,11... | collective-permute-start | bytes 786440 | tf_op jit(solution)/shard_map/ppermute | solution.py:329
  12.3 0.0 copy-start
  12.3 1.0 %copy-done = f32[2,3,2,64,128]{4,3,2,1,0:T(8,128)S(1)} copy-done((f32[2,3,2,64,128]{4,3,2,1,0:T(8,128)S(1)}, f32[2,3,2,64,128]{4,3,2,1,0:T(8,128)}, u32[]{:S(2)}) %copy-start) | copy-done | bytes 393240
  13.3 0.0 copy-start.1
  13.3 1.0 %copy-done.1 = f32[2,3,2,64,128]{4,3,2,1,0:T(8,128)S(1)} copy-done((f32[2,3,2,64,128]{4,3,2,1,0:T(8,128)S(1)}, f32[2,3,2,64,128]{4,3,2,1,0:T(8,128)}, u32[]{:S(2)}) %copy-start.1) | copy-done | bytes 393240
  14.3 0.0 copy-start.2
  14.3 0.9 %copy-done.2 = f32[2,2,64,128]{3,2,1,0:T(8,128)S(1)} copy-done((f32[2,2,64,128]{3,2,1,0:T(8,128)S(1)}, f32[2,2,64,128]{3,2,1,0:T(8,128)}, u32[]{:S(2)}) %copy-start.2) | copy-done | bytes 131096
  15.2 0.0 copy-start.3
  15.2 0.7 %copy-done.3 = s32[2,64]{1,0:T(2,128)S(1)} copy-done((s32[2,64]{1,0:T(2,128)S(1)}, s32[2,64]{1,0:T(2,128)}, u32[]{:S(2)}) %copy-start.3) | copy-done | bytes 536
  15.8 0.0 copy-start.4
  15.8 0.9 %copy-done.4 = f32[8,64,128]{2,1,0:T(8,128)S(1)} copy-done((f32[8,64,128]{2,1,0:T(8,128)S(1)}, f32[8,64,128]{2,1,0:T(8,128)}, u32[]{:S(2)}) %copy-start.4) | copy-done | bytes 262168
  16.8 0.9 %shard_map.85.kept_ref = f32[2,18,64,128]{3,2,1,0:T(8,128)S(1)} custom-call(f32[8,64,128]{2,1,0:T(8,128)S(1)} %copy-done.4, f32[2,2,64,128]{3,2,1,0:T(8,128)S(1)} %copy-done.2, f32[2,3,2,64,128]{4,3,2,1,0:T(8,128)S(1)} %copy-done, f32[2,3,2,64,128]{4,3,2,1,0:T(8,128)S(1)} %copy-done.1, s32[2,64]{1,0:T(2,128)S(1)} %copy-done.3), custom_call_target="tpu_custom_call" | custom-call | flops 10000000000 | bytes 30000000 | tf_op jit(solution)/shard_map/pallas_call | solution.py:315
  17.7 0.0 collective-permute-done.1.far_ref
  17.7 0.0 collective-permute-done.near_ref
  17.7 0.0 slice-done
  17.7 0.0 slice-done.1
  17.8 3.0 %shard_map.86 = (f32[2,2,64,128]{3,2,1,0:T(8,128)S(1)}, f32[1,256]{1,0:T(1,128)S(1)}, f32[1,256]{1,0:T(1,128)S(1)}) custom-call(f32[2,18,64,128]{3,2,1,0:T(8,128)S(1)} %shard_map.85.kept_ref, f32[8,64,128]{2,1,0:T(8,128)S(1)} %collective-permute-done.near_ref, f32[8,64,128]{2,1,0:T(8,128)S(1)} %collective-permute-done.1.far_ref, ...), custom_call_target="tpu_custom_call" | custom-call | tf_op jit(solution)/shard_map/pallas_call | solution.py:331
  20.8 0.7 %collective-permute-start.2 = (f32[1,256]{1,0:T(1,128)S(1)}, f32[1,256]{1,0:T(1,128)S(1)}, u32[]{:S(2)}, u32[]{:S(2)}) collective-permute-start(f32[1,256]{1,0:T(1,128)S(1)} %get-tuple-element.16), channel_id=1, source_target_pairs={{0,1},{1,0},{2,3},{3,2},{4,5},{5,4},{6,7},{7,6},{8,9},{9,8},{10,11... | collective-permute-start | bytes 3080 | tf_op jit(solution)/shard_map/ppermute | solution.py:338
  21.5 0.8 %collective-permute-done.2 = f32[1,256]{1,0:T(1,128)S(1)} collective-permute-done((f32[1,256]{1,0:T(1,128)S(1)}, f32[1,256]{1,0:T(1,128)S(1)}, u32[]{:S(2)}, u32[]{:S(2)}) %collective-permute-start.2) | collective-permute-done | bytes 1056 | tf_op jit(solution)/shard_map/ppermute | solution.py:338
  22.3 0.7 %broadcast_in_dim.8 = f32[128,1,256]{2,1,0:T(1,128)} broadcast(f32[256]{0:T(256)S(1)} %bitcast.9), dimensions={2} | broadcast | bytes 132096 | tf_op jit(solution)/shard_map/broadcast_in_dim | solution.py:340
  23.1 9.2 %all-to-all-start = ((f32[128,1,256]{2,1,0:T(1,128)}), f32[128,1,256]{2,1,0:T(1,128)S(1)}, u32[]{:S(2)}, u32[]{:S(2)}) async-start(f32[128,1,256]{2,1,0:T(1,128)} %broadcast_in_dim.8), calls=%async_computation | async-start | bytes 262144 | tf_op jit(solution)/shard_map/all_to_all | solution.py:341
  32.2 2.4 %collective-permute-start.6 = (f32[2,2,64,128]{3,2,1,0:T(8,128)S(1)}, f32[2,2,64,128]{3,2,1,0:T(8,128)S(1)}, u32[]{:S(2)}, u32[]{:S(2)}) collective-permute-start(f32[2,2,64,128]{3,2,1,0:T(8,128)S(1)} %get-tuple-element.17.refs_0_), channel_id=1, source_target_pairs={{0,192},{64,128},{128,64},{192,0},{1,193},{65,129},{129,65},{193,1... | collective-permute-start | bytes 393224 | tf_op jit(solution)/shard_map/ppermute | solution.py:345
  34.6 0.2 collective-permute-start.5
  34.8 0.8 %collective-permute-start.4 = (f32[2,2,64,128]{3,2,1,0:T(8,128)S(1)}, f32[2,2,64,128]{3,2,1,0:T(8,128)S(1)}, u32[]{:S(2)}, u32[]{:S(2)}) collective-permute-start(f32[2,2,64,128]{3,2,1,0:T(8,128)S(1)} %get-tuple-element.17.refs_0_), channel_id=1, source_target_pairs={{0,64},{64,0},{128,192},{192,128},{1,65},{65,1},{129,193},{193,129... | collective-permute-start | bytes 393224 | tf_op jit(solution)/shard_map/ppermute | solution.py:345
  35.6 7.6 %all-to-all-done = f32[128,1,256]{2,1,0:T(1,128)S(1)} async-done(((f32[128,1,256]{2,1,0:T(1,128)}), f32[128,1,256]{2,1,0:T(1,128)S(1)}, u32[]{:S(2)}, u32[]{:S(2)}) %all-to-all-start) | async-done | bytes 131104 | tf_op jit(solution)/shard_map/all_to_all | solution.py:341
  43.2 2.2 %collective-permute-start.3 = (f32[8,128]{1,0:T(8,128)S(1)}, f32[8,128]{1,0:T(8,128)S(1)}, u32[]{:S(2)}, u32[]{:S(2)}) collective-permute-start(f32[8,128]{1,0:T(8,128)S(1)} %bitcast.6), channel_id=1, source_target_pairs={{0,1},{1,0},{2,3},{3,2},{4,5},{5,4},{6,7},{7,6},{8,9},{9,8},{10,11... | collective-permute-start | bytes 12296 | tf_op jit(solution)/shard_map/ppermute | solution.py:343
  45.4 0.0 collective-permute-done.6.refs_3_
  45.4 0.0 collective-permute-done.5.refs_2_
  45.4 0.0 collective-permute-done.4.refs_1_
  45.4 0.8 %collective-permute-done.3.other_ref = f32[8,128]{1,0:T(8,128)S(1)} collective-permute-done((f32[8,128]{1,0:T(8,128)S(1)}, f32[8,128]{1,0:T(8,128)S(1)}, u32[]{:S(2)}, u32[]{:S(2)}) %collective-permute-start.3) | collective-permute-done | bytes 4128 | tf_op jit(solution)/shard_map/ppermute | solution.py:343
  46.2 1.2 %shard_map.87 = (f32[2,64,128]{2,1,0:T(8,128)}, f32[2,64,128]{2,1,0:T(8,128)}, f32[1,256]{1,0:T(1,128)}, f32[256,256]{1,0:T(8,128)}) custom-call(f32[8,128]{1,0:T(8,128)S(1)} %bitcast.7, f32[8,128]{1,0:T(8,128)S(1)} %collective-permute-done.3.other_ref, f32[2,2,64,128]{3,2,1,0:T(8,128)S(1)} %get-tuple-element.17.refs_0_, ...), custom_call_target="tpu_custom_call" | custom-call | tf_op jit(solution)/shard_map/pallas_call | solution.py:348
  (3 shorter events, 0.0 us)
Async XLA Ops:
  2.9 14.8 %collective-permute-start.1 = (f32[8,64,128]{2,1,0:T(8,128)}, f32[8,64,128]{2,1,0:T(8,128)S(1)}, u32[]{:S(2)}, u32[]{:S(2)}) collective-permute-start(f32[8,64,128]{2,1,0:T(8,128)} %get-tuple-element.14), channel_id=1, source_target_pairs={{0,63},{1,2},{2,1},{3,4},{4,3},{5,6},{6,5},{7,8},{8,7},{9,10},{10,... | collective-permute-start | bytes 786440 | tf_op jit(solution)/shard_map/ppermute | solution.py:324
  5.7 12.0 %slice-start = ((s8[8388608]{0:T(1024)(128)(4,1)}), s8[4194304]{0:T(1024)(128)(4,1)S(1)}, s32[]{:S(2)}) async-start(s8[8388608]{0:T(1024)(128)(4,1)} %bitcast.4), calls=%async_computation.1 | async-start | bytes 8388608
  5.7 12.1 %slice-start.1 = ((s8[8388608]{0:T(1024)(128)(4,1)}), s8[4194304]{0:T(1024)(128)(4,1)S(1)}, s32[]{:S(2)}) async-start(s8[8388608]{0:T(1024)(128)(4,1)} %bitcast.4), calls=%async_computation.2 | async-start | bytes 8388608
  5.7 12.0 %collective-permute-start = (f32[8,64,128]{2,1,0:T(8,128)}, f32[8,64,128]{2,1,0:T(8,128)S(1)}, u32[]{:S(2)}, u32[]{:S(2)}) collective-permute-start(f32[8,64,128]{2,1,0:T(8,128)} %get-tuple-element.13.after_ref), channel_id=1, source_target_pairs={{0,1},{1,0},{2,3},{3,2},{4,5},{5,4},{6,7},{7,6},{8,9},{9,8},{10,11... | collective-permute-start | bytes 786440 | tf_op jit(solution)/shard_map/ppermute | solution.py:329
  12.3 1.0 %copy-start = (f32[2,3,2,64,128]{4,3,2,1,0:T(8,128)S(1)}, f32[2,3,2,64,128]{4,3,2,1,0:T(8,128)}, u32[]{:S(2)}) copy-start(f32[2,3,2,64,128]{4,3,2,1,0:T(8,128)} %vel_hbm.3) | copy-start | bytes 1179652
  13.3 1.0 %copy-start.1 = (f32[2,3,2,64,128]{4,3,2,1,0:T(8,128)S(1)}, f32[2,3,2,64,128]{4,3,2,1,0:T(8,128)}, u32[]{:S(2)}) copy-start(f32[2,3,2,64,128]{4,3,2,1,0:T(8,128)} %disp_hbm.3) | copy-start | bytes 1179652
  14.3 0.9 %copy-start.2 = (f32[2,2,64,128]{3,2,1,0:T(8,128)S(1)}, f32[2,2,64,128]{3,2,1,0:T(8,128)}, u32[]{:S(2)}) copy-start(f32[2,2,64,128]{3,2,1,0:T(8,128)} %init_hbm.3) | copy-start | bytes 393220
  15.2 0.7 %copy-start.3 = (s32[2,64]{1,0:T(2,128)S(1)}, s32[2,64]{1,0:T(2,128)}, u32[]{:S(2)}) copy-start(s32[2,64]{1,0:T(2,128)} %bounds_hbm.3) | copy-start | bytes 1540
  15.8 0.9 %copy-start.4 = (f32[8,64,128]{2,1,0:T(8,128)S(1)}, f32[8,64,128]{2,1,0:T(8,128)}, u32[]{:S(2)}) copy-start(f32[8,64,128]{2,1,0:T(8,128)} %get-tuple-element.13.after_ref) | copy-start | bytes 786436
  20.8 1.5 %collective-permute-start.2 = (f32[1,256]{1,0:T(1,128)S(1)}, f32[1,256]{1,0:T(1,128)S(1)}, u32[]{:S(2)}, u32[]{:S(2)}) collective-permute-start(f32[1,256]{1,0:T(1,128)S(1)} %get-tuple-element.16), channel_id=1, source_target_pairs={{0,1},{1,0},{2,3},{3,2},{4,5},{5,4},{6,7},{7,6},{8,9},{9,8},{10,11... | collective-permute-start | bytes 3080 | tf_op jit(solution)/shard_map/ppermute | solution.py:338
  23.1 20.1 %all-to-all-start = ((f32[128,1,256]{2,1,0:T(1,128)}), f32[128,1,256]{2,1,0:T(1,128)S(1)}, u32[]{:S(2)}, u32[]{:S(2)}) async-start(f32[128,1,256]{2,1,0:T(1,128)} %broadcast_in_dim.8), calls=%async_computation | async-start | bytes 262144 | tf_op jit(solution)/shard_map/all_to_all | solution.py:341
  32.2 13.2 %collective-permute-start.6 = (f32[2,2,64,128]{3,2,1,0:T(8,128)S(1)}, f32[2,2,64,128]{3,2,1,0:T(8,128)S(1)}, u32[]{:S(2)}, u32[]{:S(2)}) collective-permute-start(f32[2,2,64,128]{3,2,1,0:T(8,128)S(1)} %get-tuple-element.17.refs_0_), channel_id=1, source_target_pairs={{0,192},{64,128},{128,64},{192,0},{1,193},{65,129},{129,65},{193,1... | collective-permute-start | bytes 393224 | tf_op jit(solution)/shard_map/ppermute | solution.py:345
  34.6 10.8 %collective-permute-start.5 = (f32[2,2,64,128]{3,2,1,0:T(8,128)S(1)}, f32[2,2,64,128]{3,2,1,0:T(8,128)S(1)}, u32[]{:S(2)}, u32[]{:S(2)}) collective-permute-start(f32[2,2,64,128]{3,2,1,0:T(8,128)S(1)} %get-tuple-element.17.refs_0_), channel_id=1, source_target_pairs={{0,128},{64,192},{128,0},{192,64},{1,129},{65,193},{129,1},{193,65... | collective-permute-start | bytes 393224 | tf_op jit(solution)/shard_map/ppermute | solution.py:345
  34.8 10.6 %collective-permute-start.4 = (f32[2,2,64,128]{3,2,1,0:T(8,128)S(1)}, f32[2,2,64,128]{3,2,1,0:T(8,128)S(1)}, u32[]{:S(2)}, u32[]{:S(2)}) collective-permute-start(f32[2,2,64,128]{3,2,1,0:T(8,128)S(1)} %get-tuple-element.17.refs_0_), channel_id=1, source_target_pairs={{0,64},{64,0},{128,192},{192,128},{1,65},{65,1},{129,193},{193,129... | collective-permute-start | bytes 393224 | tf_op jit(solution)/shard_map/ppermute | solution.py:345
  43.2 3.0 %collective-permute-start.3 = (f32[8,128]{1,0:T(8,128)S(1)}, f32[8,128]{1,0:T(8,128)S(1)}, u32[]{:S(2)}, u32[]{:S(2)}) collective-permute-start(f32[8,128]{1,0:T(8,128)S(1)} %bitcast.6), channel_id=1, source_target_pairs={{0,1},{1,0},{2,3},{3,2},{4,5},{5,4},{6,7},{7,6},{8,9},{9,8},{10,11... | collective-permute-start | bytes 12296 | tf_op jit(solution)/shard_map/ppermute | solution.py:343

commit v3 on v2

--- a/solution.py
+++ b/solution.py
@@ -1,5 +1,6 @@
 import jax
 import jax.numpy as jnp
+import numpy as np
 from jax import lax
 from jax.experimental import pallas as pl
 from jax.experimental.pallas import tpu as pltpu
@@ -10,6 +11,8 @@
 PACK_LIMIT = 60
 HOLD_LIMIT = 48
 HOLD_MICROS = 10
+AXES = ("real", "deep", "wide", "core")
+CELL = AXES[1:]
 
 
 def roll(a, shift, axis):
@@ -84,12 +87,13 @@
 
 
 def pack_kernel(
-    init_hbm, vel_hbm, disp_hbm, bounds_hbm, near_hbm, far_hbm,
-    init_ref, vel_ref, disp_ref, bounds_ref, near_ref, far_ref, bounds_sem, sems, out_sems,
+    init_hbm, vel_hbm, disp_hbm, bounds_hbm, far_hbm,
+    init_ref, vel_ref, disp_ref, bounds_ref, far_ref, bounds_sem, sems, out_sems,
 ):
     count, _, rows, depth = init_ref.shape
     odd = lax.axis_index("core") == 1
-    edge = lax.axis_index("chip") == jnp.where(odd, lax.axis_size("chip") - 1, 0)
+    ends_at = [jnp.where(odd, lax.axis_size(a) - 1, 0) for a in ("deep", "wide")]
+    edge = (lax.axis_index("deep") == ends_at[0]) & (lax.axis_index("wide") == ends_at[1])
     limits = pltpu.make_async_copy(bounds_hbm, bounds_ref, bounds_sem)
     limits.start()
     fields = ((init_hbm, init_ref), (vel_hbm, vel_ref), (disp_hbm, disp_ref))
@@ -105,23 +109,30 @@
     limits.wait()
     act = [activity(bounds_ref, x, rows, depth) for x in range(2)]
     last_y, last_z = ends(rows, depth)
+    side = lax.axis_index("core")
+    sign = (1 - 2 * side).astype(jnp.float32)
+    mine = jnp.where(odd, act[1], act[0])
+    inside = DT * act[0] * act[1]
     leave = []
     for r in range(count):
         for copy in arrive[r]:
             copy.wait()
-        conc, inner, along = own_terms(r, init_ref, vel_ref, disp_ref, act, last_y, last_z)
-        nxt = own_step(conc, inner, along)
-        planes = [
-            (nxt[x], conc[x], vel_ref[r, 0, x], disp_ref[r, 0, x] * act[x]) for x in range(2)
-        ]
-        for i in range(4):
-            near_ref[4 * r + i] = jnp.where(odd, planes[0][i], planes[1][i])
-            sent = jnp.where(odd, planes[1][i], planes[0][i])
-            far_ref[4 * r + i] = jnp.where(edge, 0.0, sent) if i == 3 else sent
+        inner = face(
+            vel_ref[r, 0, 0], vel_ref[r, 0, 1], disp_ref[r, 0, 0], disp_ref[r, 0, 1], inside
+        )
+        across = inner[0] * init_ref[r, 0] - inner[1] * init_ref[r, 1]
+        conc = init_ref[r, side] * mine
+        along_y = coefs(vel_ref[r, 1, side], disp_ref[r, 1, side], mine, 0, last_y)
+        along_z = coefs(vel_ref[r, 2, side], disp_ref[r, 2, side], mine, 1, last_z)
+        far_ref[4 * r] = (
+            conc - sign * across - outflow(along_y, conc, 0) - outflow(along_z, conc, 1)
+        )
+        far_ref[4 * r + 1] = conc
+        far_ref[4 * r + 2] = vel_ref[r, 0, side]
+        far_ref[4 * r + 3] = jnp.where(edge, 0.0, disp_ref[r, 0, side] * mine)
         part = pl.ds(4 * r, 4)
-        for i, (src, dst) in enumerate(((far_ref, far_hbm), (near_ref, near_hbm))):
-            leave.append(pltpu.make_async_copy(src.at[part], dst.at[part], out_sems.at[r, i]))
-            leave[-1].start()
+        leave.append(pltpu.make_async_copy(far_ref.at[part], far_hbm.at[part], out_sems.at[r]))
+        leave[-1].start()
     for copy in leave:
         copy.wait()
 
@@ -130,13 +141,14 @@
 
 
 def hold_kernel(
-    after_ref, init_hbm, vel_hbm, disp_hbm, bounds_hbm, kept_ref,
+    init_hbm, vel_hbm, disp_hbm, bounds_hbm, near_ref, kept_ref,
     init_ref, vel_ref, disp_ref, bounds_ref, sems,
 ):
     count, _, rows, depth = init_ref.shape
     pairs = [(bounds_hbm, bounds_ref), (init_hbm, init_ref)]
     pairs += [(vel_hbm, vel_ref), (disp_hbm, disp_ref)]
     fetch([pltpu.make_async_copy(src, dst, sems.at[i]) for i, (src, dst) in enumerate(pairs)])
+    odd = lax.axis_index("core") == 1
     act = [activity(bounds_ref, x, rows, depth) for x in range(2)]
     last_y, last_z = ends(rows, depth)
     for r in range(count):
@@ -152,10 +164,12 @@
                 kept_ref[r, ALONG_Z + 2 * x + i] = along[x][1][i]
         for i in range(2):
             kept_ref[r, INNER + i] = inner[i]
+        for i, planes in enumerate((NEXT, CONC, VELX, DISPX)):
+            near_ref[4 * r + i] = jnp.where(odd, kept_ref[r, planes], kept_ref[r, planes + 1])
 
 
 def step_kernel(
-    kept_ref, near_ref, far_ref, held_ref, conc_ref, mine_ref, other_ref, part_ref
+    kept_ref, near_ref, far_ref, held_ref, conc_ref, coords_ref, part_ref
 ):
     count, _, rows, depth = kept_ref.shape
     components = held_ref.shape[0]
@@ -221,11 +235,8 @@
         precision=lax.Precision.HIGHEST,
         preferred_element_type=jnp.float32,
     )
-    half = components // 2
     for r in range(count):
-        low, high = coords[r : r + 1, :half], coords[r : r + 1, half:]
-        mine_ref[:, r * half : (r + 1) * half] = jnp.where(odd, high, low)
-        other_ref[:, r * half : (r + 1) * half] = jnp.where(odd, low, high)
+        coords_ref[:, r * components : (r + 1) * components] = coords[r : r + 1]
 
 
 def tree_sum(terms):
@@ -234,15 +245,14 @@
     return terms[0]
 
 
-def stats_kernel(mine_ref, other_ref, *refs):
+def stats_kernel(parts_ref, *refs):
     fields, refs = refs[:-9], refs[-9:]
     (mean_hbm, spread_hbm, coord_hbm, cov_hbm), refs = refs[:4], refs[4:]
     mean_ref, spread_ref, coord_ref, cov_ref, sems = refs
-    odd = lax.axis_index("core") == 1
-    mine, other = mine_ref[...], other_ref[...]
-    coords = jnp.concatenate(
-        [jnp.where(odd, other, mine), jnp.where(odd, mine, other)], axis=1
-    )
+    components = coord_ref.shape[1]
+    row = tree_sum([parts_ref[i] for i in range(parts_ref.shape[0])])
+    rows = [row[:, j : j + components] for j in range(0, row.shape[1], components)]
+    coords = jnp.concatenate(rows, axis=0)
     number = coords.shape[0]
     mean = jnp.sum(coords, axis=0, keepdims=True) * (1.0 / number)
     coord_ref[...] = mean
@@ -291,8 +301,7 @@
 def shards(initial, velocity, dispersion, bounds, basis):
     count, width, rows, depth = initial.shape
     components = basis.shape[0]
-    half = components // 2
-    reals, chips, _ = (lax.axis_size(a) for a in ("real", "chip", "core"))
+    reals, deep, wide, cores = (lax.axis_size(a) for a in AXES)
     f32 = jnp.float32
     vmem = pltpu.VMEM
 
@@ -302,45 +311,51 @@
     inputs = (initial, velocity, dispersion, bounds)
     own = [pltpu.VMEM(a.shape, a.dtype) for a in inputs]
     dma = pltpu.SemaphoreType.DMA
-    near, far = call(
+    far = call(
         pack_kernel,
-        (packed, packed),
+        packed,
         [hbm] * 4,
         own
-        + [pltpu.VMEM(packed.shape, f32)] * 2
-        + [dma(()), dma((count, 3)), dma((count, 2))],
+        + [pltpu.VMEM(packed.shape, f32)]
+        + [dma(()), dma((count, 3)), dma((count,))],
         PACK_LIMIT,
+        HOLD_MICROS,
         out=hbm,
     )(*inputs)
-    kept = call(
+    near, kept = call(
         hold_kernel,
-        jax.ShapeDtypeStruct((count, PLANES, *plane), f32),
-        [pl.ANY] + [hbm] * 4,
+        (packed, jax.ShapeDtypeStruct((count, PLANES, *plane), f32)),
+        [hbm] * 4,
         own + [dma((4,))],
         HOLD_LIMIT,
         HOLD_MICROS,
-    )(near, *inputs)
-    cells = 2 * chips
-    far = lax.ppermute(
-        far,
-        ("chip", "core"),
-        [(i, ((i + 1) ^ 1) - 1 if 0 < i < cells - 1 else cells - 1 - i) for i in range(cells)],
-    )
+    )(*inputs)
+    cells = deep * wide * cores
+    pairs = [
+        (r * cells + i, r * cells + ((i + 1) ^ 1) - 1 if 0 < i < cells - 1 else (r ^ 1) * cells + i)
+        for r in range(reals)
+        for i in range(cells)
+    ]
+    far = lax.ppermute(far, AXES, pairs)
     near = lax.ppermute(near, "core", [(0, 1), (1, 0)])
-    line = jax.ShapeDtypeStruct((1, count * half), f32)
-    conc, mine, other = call(
+    line = (1, count * components)
+    conc, coords = call(
         step_kernel,
-        (jax.ShapeDtypeStruct(initial.shape, f32), line, line),
+        (jax.ShapeDtypeStruct(initial.shape, f32), jax.ShapeDtypeStruct(line, f32)),
         [vmem] * 4,
         [pltpu.VMEM((components * 8, count * rows), f32)],
     )(kept, near, far, basis)
 
-    mine = mine + lax.ppermute(other, "core", [(0, 1), (1, 0)])
-    spots = reals * chips
-    sent = jnp.broadcast_to(mine.reshape(1, 1, count * half), (spots, 1, count * half))
-    got = lax.all_to_all(sent, ("real", "chip"), 0, 0, tiled=True)
-    mine = got.reshape(reals, chips, count, half).sum(axis=1).reshape(reals * count, half)
-    other = lax.ppermute(mine, "core", [(0, 1), (1, 0)])
+    everything = np.arange(reals * cells).reshape(reals, deep, wide * cores)
+
+    def spread_out(a, groups):
+        sent = jnp.broadcast_to(a[None], (groups.shape[1], *a.shape))
+        groups = groups[:, ::-1].tolist()
+        return lax.all_to_all(sent, AXES, 0, 0, axis_index_groups=groups, tiled=True)
+
+    parts = spread_out(coords, everything.transpose(1, 0, 2).reshape(deep, -1))
+    coords = parts.reshape(reals, wide * cores, -1).sum(axis=1).reshape(1, -1)
+    parts = spread_out(coords, everything.transpose(0, 2, 1).reshape(-1, deep))
     fields = [conc] + [
         lax.ppermute(conc, "real", [(i, i ^ k) for i in range(reals)]) for k in range(1, reals)
     ]
@@ -348,27 +363,26 @@
     mean_field, spread_field, coord_mean, coord_cov = call(
         stats_kernel,
         tuple(jax.ShapeDtypeStruct(a, f32) for a in shapes),
-        [vmem] * (2 + reals),
+        [vmem] * (1 + reals),
         [pltpu.VMEM(a, f32) for a in shapes] + [dma((4,))],
         out=hbm,
-    )(mine, other, *fields)
+    )(parts, *fields)
     return mean_field, spread_field, coord_mean.reshape(components), coord_cov
 
 
 def solution(mesh):
     reals, cells = mesh.devices.shape
-    split = Mesh(mesh.devices.reshape(reals, cells // 2, 2), ("real", "chip", "core"))
-    cell = ("chip", "core")
+    split = Mesh(mesh.devices.reshape(reals, cells // 8, 4, 2), AXES)
     return jax.shard_map(
         shards,
         mesh=split,
         in_specs=(
-            P("real", cell, None, None),
-            P("real", None, cell, None, None),
-            P("real", None, cell, None, None),
-            P(cell, None),
-            P(None, cell, None, None),
+            P("real", CELL, None, None),
+            P("real", None, CELL, None, None),
+            P("real", None, CELL, None, None),
+            P(CELL, None),
+            P(None, CELL, None, None),
         ),
-        out_specs=(P(cell, None, None), P(cell, None, None), P(), P()),
+        out_specs=(P(CELL, None, None), P(CELL, None, None), P(), P()),
         check_vma=False,
     )

time: 47.7 us -> 44 us (0.922)
  local copies, waits for them, and re-layouts: 5.26 us -> 1.39 us
  starting transfers between devices: 24.7 us -> 26.4 us
  waiting for transfers between devices: 9.24 us -> 7.79 us
    all_to_all x1 -> x2, starting transfers between devices: 9.16 us -> 19.6 us  [spread_out(): lax.all_to_all(sent, AXES, 0, 0, axis_index_groups=groups, tiled=True)]
    ppermute x1, starting transfers between devices: 6.56 us -> 0.68 us  [shards(): near = lax.ppermute(near, 'core', [(0, 1), (1, 0)])]
    unnamed x14 -> x11, local copies, waits for them, and re-layouts: 4.53 us -> 0.03 us
    ppermute x3 -> x1, starting transfers between devices: 5.68 us -> 2.77 us  [shards(): far = lax.ppermute(far, AXES, pairs)]
    all_to_all x1 -> x2, waiting for transfers between devices: 7.6 us -> 4.85 us  [spread_out(): lax.all_to_all(sent, AXES, 0, 0, axis_index_groups=groups, tiled=True)]
    ppermute x3 -> x1, waiting for transfers between devices: 1.63 us -> 2.92 us  [shards(): far = lax.ppermute(far, AXES, pairs)]
    broadcast_in_dim x1 -> x2, local copies, waits for them, and re-layouts: 0.73 us -> 1.36 us  [spread_out(): sent = jnp.broadcast_to(a[None], (groups.shape[1], *a.shape))]
  transfers between devices with their start and end apart: 8 -> 7, of which waited for: 3 -> 3; matrix products, arithmetic and copies ran while one was open for 0% -> 2% of each run, Pallas kernels for 2% -> 2%
where the time goes in v3:
time: 44 us; the launch traced here: 43.7 us
  starting transfers between devices  26.4 us (60%)
  waiting for transfers between devices  7.79 us (18%)
  Pallas kernels  7.4 us (17%)
  local copies, waits for them, and re-layouts  1.39 us (3%)
  between operations  0.72 us (2%)
    all_to_all x2, starting transfers between devices, spread_out(): lax.all_to_all(sent, AXES, 0, 0, axis_index_groups=groups, tiled=True)  19.6 us
    all_to_all x2, waiting for transfers between devices, spread_out(): lax.all_to_all(sent, AXES, 0, 0, axis_index_groups=groups, tiled=True)  4.85 us
    ppermute x3, starting transfers between devices, shards(): lax.ppermute(conc, 'real', [(i, i ^ k) for i in range(reals)])  3.34 us
    pallas_call x1, Pallas kernels, shards(): call(step_kernel, (jax.ShapeDtypeStruct(initial.shape, f32), jax.ShapeDty...  2.99 us
    ppermute x1, waiting for transfers between devices, shards(): far = lax.ppermute(far, AXES, pairs)  2.92 us
    ppermute x1, starting transfers between devices, shards(): far = lax.ppermute(far, AXES, pairs)  2.77 us
    pallas_call x1, Pallas kernels, shards(): call(pack_kernel, packed, [hbm] * 4, own + [pltpu.VMEM(packed.shape, f32)...  2.23 us
    broadcast_in_dim x2, local copies, waits for them, and re-layouts, spread_out(): sent = jnp.broadcast_to(a[None], (groups.shape[1], *a.shape))  1.36 us
  transfers between devices with their start and end apart: 7, of which 3 were waited for; matrix products, arithmetic and copies ran while one was open for 2% of the time, Pallas kernels for 2%

profile of v3, /device:TPU:1, one launch (start us, length us, event | category | flops | bytes accessed | tf_op | source)
XLA Modules:
  0.0 43.7 jit_solution(8761873018986109147)
XLA Ops:
  0.6 0.0 copy-start.4
  0.6 0.0 copy-start.2
  0.7 0.0 copy-start.1
  0.7 0.0 copy-start.3
  0.7 2.2 %shard_map.85 = f32[8,64,128]{2,1,0:T(8,128)} custom-call(f32[2,2,64,128]{3,2,1,0:T(8,128)} %init_hbm.3, f32[2,3,2,64,128]{4,3,2,1,0:T(8,128)} %vel_hbm.3, f32[2,3,2,64,128]{4,3,2,1,0:T(8,128)} %disp_hbm.3, s32[2,64]{1,0:T(2,128)} %bounds_hbm.3), custom_call_target="tpu_custom_call" | custom-call | flops 10000000000 | bytes 30000000 | tf_op jit(solution)/shard_map/pallas_call | solution.py:314
  2.9 0.0 copy-start
  2.9 2.8 %collective-permute-start.1 = (f32[8,64,128]{2,1,0:T(8,128)}, f32[8,64,128]{2,1,0:T(8,128)S(1)}, u32[]{:S(2)}, u32[]{:S(2)}) collective-permute-start(f32[8,64,128]{2,1,0:T(8,128)} %shard_map.85), channel_id=1, source_target_pairs={{0,64},{1,2},{2,1},{3,4},{4,3},{5,6},{6,5},{7,8},{8,7},{9,10},{10,... | collective-permute-start | bytes 786440 | tf_op jit(solution)/shard_map/ppermute | solution.py:339
  5.7 0.0 copy-done.4
  5.7 0.0 copy-done.2
  5.7 0.0 copy-done.1
  5.7 0.0 copy-done.3
  5.7 0.9 %shard_map.84 = (f32[8,64,128]{2,1,0:T(8,128)S(1)}, f32[2,18,64,128]{3,2,1,0:T(8,128)S(1)}) custom-call(f32[2,2,64,128]{3,2,1,0:T(8,128)S(1)} %copy-done.3, f32[2,3,2,64,128]{4,3,2,1,0:T(8,128)S(1)} %copy-done.1, f32[2,3,2,64,128]{4,3,2,1,0:T(8,128)S(1)} %copy-done.2, s32[2,64]{1,0:T(2,128)S(1)} %copy-done.4), custom_call_target="tpu_custom_call" | custom-call | flops 10000000000 | bytes 30000000 | tf_op jit(solution)/shard_map/pallas_call | solution.py:325
  6.7 0.7 %collective-permute-start = (f32[8,64,128]{2,1,0:T(8,128)S(1)}, f32[8,64,128]{2,1,0:T(8,128)S(1)}, u32[]{:S(2)}, u32[]{:S(2)}) collective-permute-start(f32[8,64,128]{2,1,0:T(8,128)S(1)} %get-tuple-element.13), channel_id=1, source_target_pairs={{0,1},{1,0},{2,3},{3,2},{4,5},{5,4},{6,7},{7,6},{8,9},{9,8},{10,11... | collective-permute-start | bytes 786440 | tf_op jit(solution)/shard_map/ppermute | solution.py:340
  7.3 2.9 %collective-permute-done.1.far_ref = f32[8,64,128]{2,1,0:T(8,128)S(1)} collective-permute-done((f32[8,64,128]{2,1,0:T(8,128)}, f32[8,64,128]{2,1,0:T(8,128)S(1)}, u32[]{:S(2)}, u32[]{:S(2)}) %collective-permute-start.1) | collective-permute-done | bytes 262176 | tf_op jit(solution)/shard_map/ppermute | solution.py:339
  10.3 0.0 collective-permute-done.near_ref
  10.3 0.0 copy-done
  10.3 3.0 %shard_map.86 = (f32[2,2,64,128]{3,2,1,0:T(8,128)S(1)}, f32[1,512]{1,0:T(1,128)S(1)}) custom-call(f32[2,18,64,128]{3,2,1,0:T(8,128)S(1)} %get-tuple-element.12.kept_ref, f32[8,64,128]{2,1,0:T(8,128)S(1)} %collective-permute-done.near_ref, f32[8,64,128]{2,1,0:T(8,128)S(1)} %collective-permute-done.1.far_ref, bf16[256,2,64,128]{3,2,1,0:T(8,128)(2,1)S(1)} %copy-done), custom_call_target="tpu_custom_call" | custom-call | tf_op jit(solution)/shard_map/pallas_call | solution.py:342
  13.3 0.7 %broadcast_in_dim.16 = f32[32,1,512]{2,1,0:T(1,128)} broadcast(f32[512]{0:T(512)S(1)} %bitcast.6), dimensions={2} | broadcast | bytes 67584 | tf_op jit(solution)/shard_map/broadcast_in_dim | solution.py:352
  14.0 10.3 %all-to-all-start = ((f32[32,1,512]{2,1,0:T(1,128)}), f32[32,1,512]{2,1,0:T(1,128)S(1)}, u32[]{:S(2)}, u32[]{:S(2)}) async-start(f32[32,1,512]{2,1,0:T(1,128)} %broadcast_in_dim.16), calls=%async_computation | async-start | bytes 131072 | tf_op jit(solution)/shard_map/all_to_all | solution.py:354
  24.3 0.2 collective-permute-start.4
  24.5 2.2 %collective-permute-start.3 = (f32[2,2,64,128]{3,2,1,0:T(8,128)S(1)}, f32[2,2,64,128]{3,2,1,0:T(8,128)S(1)}, u32[]{:S(2)}, u32[]{:S(2)}) collective-permute-start(f32[2,2,64,128]{3,2,1,0:T(8,128)S(1)} %get-tuple-element.15.refs_0_), channel_id=1, source_target_pairs={{0,128},{64,192},{128,0},{192,64},{1,129},{65,193},{129,1},{193,65... | collective-permute-start | bytes 393224 | tf_op jit(solution)/shard_map/ppermute | solution.py:360
  26.7 0.9 %collective-permute-start.2 = (f32[2,2,64,128]{3,2,1,0:T(8,128)S(1)}, f32[2,2,64,128]{3,2,1,0:T(8,128)S(1)}, u32[]{:S(2)}, u32[]{:S(2)}) collective-permute-start(f32[2,2,64,128]{3,2,1,0:T(8,128)S(1)} %get-tuple-element.15.refs_0_), channel_id=1, source_target_pairs={{0,64},{64,0},{128,192},{192,128},{1,65},{65,1},{129,193},{193,129... | collective-permute-start | bytes 393224 | tf_op jit(solution)/shard_map/ppermute | solution.py:360
  27.6 0.3 all-to-all-done
  28.0 0.7 %broadcast_in_dim.18 = f32[8,1,2048]{2,1,0:T(1,128)} broadcast(f32[2048]{0:T(1024)S(1)} %bitcast.8), dimensions={2} | broadcast | bytes 73728 | tf_op jit(solution)/shard_map/broadcast_in_dim | solution.py:352
  28.6 9.2 %all-to-all-start.1 = ((f32[8,1,2048]{2,1,0:T(1,128)}), f32[8,1,2048]{2,1,0:T(1,128)S(1)}, u32[]{:S(2)}, u32[]{:S(2)}) async-start(f32[8,1,2048]{2,1,0:T(1,128)} %broadcast_in_dim.18), calls=%async_computation.1 | async-start | bytes 131072 | tf_op jit(solution)/shard_map/all_to_all | solution.py:354
  37.9 0.0 collective-permute-done.4.refs_3_
  37.9 0.0 collective-permute-done.3.refs_2_
  37.9 0.0 collective-permute-done.2.refs_1_
  37.9 4.6 %all-to-all-done.1.parts_ref = f32[8,1,2048]{2,1,0:T(1,128)S(1)} async-done(((f32[8,1,2048]{2,1,0:T(1,128)}), f32[8,1,2048]{2,1,0:T(1,128)S(1)}, u32[]{:S(2)}, u32[]{:S(2)}) %all-to-all-start.1) | async-done | bytes 65568 | tf_op jit(solution)/shard_map/all_to_all | solution.py:354
  42.4 1.2 %shard_map.87 = (f32[2,64,128]{2,1,0:T(8,128)}, f32[2,64,128]{2,1,0:T(8,128)}, f32[1,256]{1,0:T(1,128)}, f32[256,256]{1,0:T(8,128)}) custom-call(f32[8,1,2048]{2,1,0:T(1,128)S(1)} %all-to-all-done.1.parts_ref, f32[2,2,64,128]{3,2,1,0:T(8,128)S(1)} %get-tuple-element.15.refs_0_, f32[2,2,64,128]{3,2,1,0:T(8,128)S(1)} %collective-permute-done.2.refs_1_, ...), custom_call_target="tpu_custom_call" | custom-call | tf_op jit(solution)/shard_map/pallas_call | solution.py:363
  (2 shorter events, 0.0 us)
Async XLA Ops:
  0.6 5.1 %copy-start.4 = (s32[2,64]{1,0:T(2,128)S(1)}, s32[2,64]{1,0:T(2,128)}, u32[]{:S(2)}) copy-start(s32[2,64]{1,0:T(2,128)} %bounds_hbm.3) | copy-start | bytes 1540
  0.6 5.1 %copy-start.2 = (f32[2,3,2,64,128]{4,3,2,1,0:T(8,128)S(1)}, f32[2,3,2,64,128]{4,3,2,1,0:T(8,128)}, u32[]{:S(2)}) copy-start(f32[2,3,2,64,128]{4,3,2,1,0:T(8,128)} %disp_hbm.3) | copy-start | bytes 1179652
  0.7 5.1 %copy-start.1 = (f32[2,3,2,64,128]{4,3,2,1,0:T(8,128)S(1)}, f32[2,3,2,64,128]{4,3,2,1,0:T(8,128)}, u32[]{:S(2)}) copy-start(f32[2,3,2,64,128]{4,3,2,1,0:T(8,128)} %vel_hbm.3) | copy-start | bytes 1179652
  0.7 5.0 %copy-start.3 = (f32[2,2,64,128]{3,2,1,0:T(8,128)S(1)}, f32[2,2,64,128]{3,2,1,0:T(8,128)}, u32[]{:S(2)}) copy-start(f32[2,2,64,128]{3,2,1,0:T(8,128)} %init_hbm.3) | copy-start | bytes 393220
  2.9 7.4 %copy-start = (bf16[256,2,64,128]{3,2,1,0:T(8,128)(2,1)S(1)}, bf16[256,2,64,128]{3,2,1,0:T(8,128)(2,1)}, u32[]{:S(2)}) copy-start(bf16[256,2,64,128]{3,2,1,0:T(8,128)(2,1)} %held_ref.1) | copy-start | bytes 25165828
  2.9 7.3 %collective-permute-start.1 = (f32[8,64,128]{2,1,0:T(8,128)}, f32[8,64,128]{2,1,0:T(8,128)S(1)}, u32[]{:S(2)}, u32[]{:S(2)}) collective-permute-start(f32[8,64,128]{2,1,0:T(8,128)} %shard_map.85), channel_id=1, source_target_pairs={{0,64},{1,2},{2,1},{3,4},{4,3},{5,6},{6,5},{7,8},{8,7},{9,10},{10,... | collective-permute-start | bytes 786440 | tf_op jit(solution)/shard_map/ppermute | solution.py:339
  6.7 3.6 %collective-permute-start = (f32[8,64,128]{2,1,0:T(8,128)S(1)}, f32[8,64,128]{2,1,0:T(8,128)S(1)}, u32[]{:S(2)}, u32[]{:S(2)}) collective-permute-start(f32[8,64,128]{2,1,0:T(8,128)S(1)} %get-tuple-element.13), channel_id=1, source_target_pairs={{0,1},{1,0},{2,3},{3,2},{4,5},{5,4},{6,7},{7,6},{8,9},{9,8},{10,11... | collective-permute-start | bytes 786440 | tf_op jit(solution)/shard_map/ppermute | solution.py:340
  14.0 14.0 %all-to-all-start = ((f32[32,1,512]{2,1,0:T(1,128)}), f32[32,1,512]{2,1,0:T(1,128)S(1)}, u32[]{:S(2)}, u32[]{:S(2)}) async-start(f32[32,1,512]{2,1,0:T(1,128)} %broadcast_in_dim.16), calls=%async_computation | async-start | bytes 131072 | tf_op jit(solution)/shard_map/all_to_all | solution.py:354
  24.3 13.6 %collective-permute-start.4 = (f32[2,2,64,128]{3,2,1,0:T(8,128)S(1)}, f32[2,2,64,128]{3,2,1,0:T(8,128)S(1)}, u32[]{:S(2)}, u32[]{:S(2)}) collective-permute-start(f32[2,2,64,128]{3,2,1,0:T(8,128)S(1)} %get-tuple-element.15.refs_0_), channel_id=1, source_target_pairs={{0,192},{64,128},{128,64},{192,0},{1,193},{65,129},{129,65},{193,1... | collective-permute-start | bytes 393224 | tf_op jit(solution)/shard_map/ppermute | solution.py:360
  24.5 13.4 %collective-permute-start.3 = (f32[2,2,64,128]{3,2,1,0:T(8,128)S(1)}, f32[2,2,64,128]{3,2,1,0:T(8,128)S(1)}, u32[]{:S(2)}, u32[]{:S(2)}) collective-permute-start(f32[2,2,64,128]{3,2,1,0:T(8,128)S(1)} %get-tuple-element.15.refs_0_), channel_id=1, source_target_pairs={{0,128},{64,192},{128,0},{192,64},{1,129},{65,193},{129,1},{193,65... | collective-permute-start | bytes 393224 | tf_op jit(solution)/shard_map/ppermute | solution.py:360
  26.7 11.2 %collective-permute-start.2 = (f32[2,2,64,128]{3,2,1,0:T(8,128)S(1)}, f32[2,2,64,128]{3,2,1,0:T(8,128)S(1)}, u32[]{:S(2)}, u32[]{:S(2)}) collective-permute-start(f32[2,2,64,128]{3,2,1,0:T(8,128)S(1)} %get-tuple-element.15.refs_0_), channel_id=1, source_target_pairs={{0,64},{64,0},{128,192},{192,128},{1,65},{65,1},{129,193},{193,129... | collective-permute-start | bytes 393224 | tf_op jit(solution)/shard_map/ppermute | solution.py:360
  28.6 13.8 %all-to-all-start.1 = ((f32[8,1,2048]{2,1,0:T(1,128)}), f32[8,1,2048]{2,1,0:T(1,128)S(1)}, u32[]{:S(2)}, u32[]{:S(2)}) async-start(f32[8,1,2048]{2,1,0:T(1,128)} %broadcast_in_dim.18), calls=%async_computation.1 | async-start | bytes 131072 | tf_op jit(solution)/shard_map/all_to_all | solution.py:354

commit v4 on v3

--- a/solution.py
+++ b/solution.py
@@ -350,12 +350,13 @@
 
     def spread_out(a, groups):
         sent = jnp.broadcast_to(a[None], (groups.shape[1], *a.shape))
-        groups = groups[:, ::-1].tolist()
-        return lax.all_to_all(sent, AXES, 0, 0, axis_index_groups=groups, tiled=True)
-
-    parts = spread_out(coords, everything.transpose(1, 0, 2).reshape(deep, -1))
+        return lax.all_to_all(sent, AXES, 0, 0, axis_index_groups=groups.tolist(), tiled=True)
+
+    parts = spread_out(coords, everything.transpose(1, 0, 2).reshape(deep, -1)[:, ::-1])
     coords = parts.reshape(reals, wide * cores, -1).sum(axis=1).reshape(1, -1)
-    parts = spread_out(coords, everything.transpose(0, 2, 1).reshape(-1, deep))
+    parts = spread_out(
+        coords, np.roll(everything.transpose(0, 2, 1).reshape(-1, deep), deep // 2, axis=1)
+    )
     fields = [conc] + [
         lax.ppermute(conc, "real", [(i, i ^ k) for i in range(reals)]) for k in range(1, reals)
     ]

time: 44 us -> 43.1 us (0.980)
  waiting for transfers between devices: 7.79 us -> 5.63 us
  starting transfers between devices: 26.4 us -> 27.7 us
    all_to_all x2, waiting for transfers between devices: 4.85 us -> 2.7 us  [spread_out(): lax.all_to_all(sent, AXES, 0, 0, axis_index_groups=groups.tolist(), tiled...]
    all_to_all x2, starting transfers between devices: 19.6 us -> 20.9 us  [spread_out(): lax.all_to_all(sent, AXES, 0, 0, axis_index_groups=groups.tolist(), tiled...]
where the time goes in v4:
time: 43.1 us; the launch traced here: 42.9 us
  starting transfers between devices  27.7 us (64%)
  Pallas kernels  7.4 us (17%)
  waiting for transfers between devices  5.63 us (13%)
  local copies, waits for them, and re-layouts  1.39 us (3%)
  between operations  0.72 us (2%)
    all_to_all x2, starting transfers between devices, spread_out(): lax.all_to_all(sent, AXES, 0, 0, axis_index_groups=groups.tolist(), tiled...  20.9 us
    ppermute x3, starting transfers between devices, shards(): lax.ppermute(conc, 'real', [(i, i ^ k) for i in range(reals)])  3.34 us
    pallas_call x1, Pallas kernels, shards(): call(step_kernel, (jax.ShapeDtypeStruct(initial.shape, f32), jax.ShapeDty...  2.99 us
    ppermute x1, waiting for transfers between devices, shards(): far = lax.ppermute(far, AXES, pairs)  2.92 us
    ppermute x1, starting transfers between devices, shards(): far = lax.ppermute(far, AXES, pairs)  2.77 us
    all_to_all x2, waiting for transfers between devices, spread_out(): lax.all_to_all(sent, AXES, 0, 0, axis_index_groups=groups.tolist(), tiled...  2.7 us
    pallas_call x1, Pallas kernels, shards(): call(pack_kernel, packed, [hbm] * 4, own + [pltpu.VMEM(packed.shape, f32)...  2.23 us
    broadcast_in_dim x2, local copies, waits for them, and re-layouts, spread_out(): sent = jnp.broadcast_to(a[None], (groups.shape[1], *a.shape))  1.36 us
  transfers between devices with their start and end apart: 7, of which 3 were waited for; matrix products, arithmetic and copies ran while one was open for 2% of the time, Pallas kernels for 2%

profile of v4, /device:TPU:1, one launch (start us, length us, event | category | flops | bytes accessed | tf_op | source)
XLA Modules:
  0.0 42.9 jit_solution(4481018518891592158)
XLA Ops:
  0.6 0.0 copy-start.4
  0.6 0.0 copy-start.2
  0.7 0.0 copy-start.1
  0.7 0.0 copy-start.3
  0.7 2.2 %shard_map.85 = f32[8,64,128]{2,1,0:T(8,128)} custom-call(f32[2,2,64,128]{3,2,1,0:T(8,128)} %init_hbm.3, f32[2,3,2,64,128]{4,3,2,1,0:T(8,128)} %vel_hbm.3, f32[2,3,2,64,128]{4,3,2,1,0:T(8,128)} %disp_hbm.3, s32[2,64]{1,0:T(2,128)} %bounds_hbm.3), custom_call_target="tpu_custom_call" | custom-call | flops 10000000000 | bytes 30000000 | tf_op jit(solution)/shard_map/pallas_call | solution.py:314
  2.9 0.0 copy-start
  2.9 2.8 %collective-permute-start.1 = (f32[8,64,128]{2,1,0:T(8,128)}, f32[8,64,128]{2,1,0:T(8,128)S(1)}, u32[]{:S(2)}, u32[]{:S(2)}) collective-permute-start(f32[8,64,128]{2,1,0:T(8,128)} %shard_map.85), channel_id=1, source_target_pairs={{0,64},{1,2},{2,1},{3,4},{4,3},{5,6},{6,5},{7,8},{8,7},{9,10},{10,... | collective-permute-start | bytes 786440 | tf_op jit(solution)/shard_map/ppermute | solution.py:339
  5.7 0.0 copy-done.4
  5.7 0.0 copy-done.2
  5.7 0.0 copy-done.1
  5.7 0.0 copy-done.3
  5.7 0.9 %shard_map.84 = (f32[8,64,128]{2,1,0:T(8,128)S(1)}, f32[2,18,64,128]{3,2,1,0:T(8,128)S(1)}) custom-call(f32[2,2,64,128]{3,2,1,0:T(8,128)S(1)} %copy-done.3, f32[2,3,2,64,128]{4,3,2,1,0:T(8,128)S(1)} %copy-done.1, f32[2,3,2,64,128]{4,3,2,1,0:T(8,128)S(1)} %copy-done.2, s32[2,64]{1,0:T(2,128)S(1)} %copy-done.4), custom_call_target="tpu_custom_call" | custom-call | flops 10000000000 | bytes 30000000 | tf_op jit(solution)/shard_map/pallas_call | solution.py:325
  6.7 0.7 %collective-permute-start = (f32[8,64,128]{2,1,0:T(8,128)S(1)}, f32[8,64,128]{2,1,0:T(8,128)S(1)}, u32[]{:S(2)}, u32[]{:S(2)}) collective-permute-start(f32[8,64,128]{2,1,0:T(8,128)S(1)} %get-tuple-element.13), channel_id=1, source_target_pairs={{0,1},{1,0},{2,3},{3,2},{4,5},{5,4},{6,7},{7,6},{8,9},{9,8},{10,11... | collective-permute-start | bytes 786440 | tf_op jit(solution)/shard_map/ppermute | solution.py:340
  7.3 2.9 %collective-permute-done.1.far_ref = f32[8,64,128]{2,1,0:T(8,128)S(1)} collective-permute-done((f32[8,64,128]{2,1,0:T(8,128)}, f32[8,64,128]{2,1,0:T(8,128)S(1)}, u32[]{:S(2)}, u32[]{:S(2)}) %collective-permute-start.1) | collective-permute-done | bytes 262176 | tf_op jit(solution)/shard_map/ppermute | solution.py:339
  10.3 0.0 collective-permute-done.near_ref
  10.3 0.0 copy-done
  10.3 3.0 %shard_map.86 = (f32[2,2,64,128]{3,2,1,0:T(8,128)S(1)}, f32[1,512]{1,0:T(1,128)S(1)}) custom-call(f32[2,18,64,128]{3,2,1,0:T(8,128)S(1)} %get-tuple-element.12.kept_ref, f32[8,64,128]{2,1,0:T(8,128)S(1)} %collective-permute-done.near_ref, f32[8,64,128]{2,1,0:T(8,128)S(1)} %collective-permute-done.1.far_ref, bf16[256,2,64,128]{3,2,1,0:T(8,128)(2,1)S(1)} %copy-done), custom_call_target="tpu_custom_call" | custom-call | tf_op jit(solution)/shard_map/pallas_call | solution.py:342
  13.3 0.7 %broadcast_in_dim.16 = f32[32,1,512]{2,1,0:T(1,128)} broadcast(f32[512]{0:T(512)S(1)} %bitcast.6), dimensions={2} | broadcast | bytes 67584 | tf_op jit(solution)/shard_map/broadcast_in_dim | solution.py:352
  14.0 10.3 %all-to-all-start = ((f32[32,1,512]{2,1,0:T(1,128)}), f32[32,1,512]{2,1,0:T(1,128)S(1)}, u32[]{:S(2)}, u32[]{:S(2)}) async-start(f32[32,1,512]{2,1,0:T(1,128)} %broadcast_in_dim.16), calls=%async_computation | async-start | bytes 131072 | tf_op jit(solution)/shard_map/all_to_all | solution.py:353
  24.3 0.2 collective-permute-start.4
  24.5 2.2 %collective-permute-start.3 = (f32[2,2,64,128]{3,2,1,0:T(8,128)S(1)}, f32[2,2,64,128]{3,2,1,0:T(8,128)S(1)}, u32[]{:S(2)}, u32[]{:S(2)}) collective-permute-start(f32[2,2,64,128]{3,2,1,0:T(8,128)S(1)} %get-tuple-element.15.refs_0_), channel_id=1, source_target_pairs={{0,128},{64,192},{128,0},{192,64},{1,129},{65,193},{129,1},{193,65... | collective-permute-start | bytes 393224 | tf_op jit(solution)/shard_map/ppermute | solution.py:361
  26.7 0.9 %collective-permute-start.2 = (f32[2,2,64,128]{3,2,1,0:T(8,128)S(1)}, f32[2,2,64,128]{3,2,1,0:T(8,128)S(1)}, u32[]{:S(2)}, u32[]{:S(2)}) collective-permute-start(f32[2,2,64,128]{3,2,1,0:T(8,128)S(1)} %get-tuple-element.15.refs_0_), channel_id=1, source_target_pairs={{0,64},{64,0},{128,192},{192,128},{1,65},{65,1},{129,193},{193,129... | collective-permute-start | bytes 393224 | tf_op jit(solution)/shard_map/ppermute | solution.py:361
  27.6 0.3 all-to-all-done
  28.0 0.7 %broadcast_in_dim.18 = f32[8,1,2048]{2,1,0:T(1,128)} broadcast(f32[2048]{0:T(1024)S(1)} %bitcast.8), dimensions={2} | broadcast | bytes 73728 | tf_op jit(solution)/shard_map/broadcast_in_dim | solution.py:352
  28.6 10.6 %all-to-all-start.1 = ((f32[8,1,2048]{2,1,0:T(1,128)}), f32[8,1,2048]{2,1,0:T(1,128)S(1)}, u32[]{:S(2)}, u32[]{:S(2)}) async-start(f32[8,1,2048]{2,1,0:T(1,128)} %broadcast_in_dim.18), calls=%async_computation.1 | async-start | bytes 131072 | tf_op jit(solution)/shard_map/all_to_all | solution.py:353
  39.2 0.0 collective-permute-done.4.refs_3_
  39.3 0.0 collective-permute-done.3.refs_2_
  39.3 0.0 collective-permute-done.2.refs_1_
  39.3 2.4 %all-to-all-done.1.parts_ref = f32[8,1,2048]{2,1,0:T(1,128)S(1)} async-done(((f32[8,1,2048]{2,1,0:T(1,128)}), f32[8,1,2048]{2,1,0:T(1,128)S(1)}, u32[]{:S(2)}, u32[]{:S(2)}) %all-to-all-start.1) | async-done | bytes 65568 | tf_op jit(solution)/shard_map/all_to_all | solution.py:353
  41.7 1.2 %shard_map.87 = (f32[2,64,128]{2,1,0:T(8,128)}, f32[2,64,128]{2,1,0:T(8,128)}, f32[1,256]{1,0:T(1,128)}, f32[256,256]{1,0:T(8,128)}) custom-call(f32[8,1,2048]{2,1,0:T(1,128)S(1)} %all-to-all-done.1.parts_ref, f32[2,2,64,128]{3,2,1,0:T(8,128)S(1)} %get-tuple-element.15.refs_0_, f32[2,2,64,128]{3,2,1,0:T(8,128)S(1)} %collective-permute-done.2.refs_1_, ...), custom_call_target="tpu_custom_call" | custom-call | tf_op jit(solution)/shard_map/pallas_call | solution.py:364
  (2 shorter events, 0.0 us)
Async XLA Ops:
  0.6 5.1 %copy-start.4 = (s32[2,64]{1,0:T(2,128)S(1)}, s32[2,64]{1,0:T(2,128)}, u32[]{:S(2)}) copy-start(s32[2,64]{1,0:T(2,128)} %bounds_hbm.3) | copy-start | bytes 1540
  0.6 5.1 %copy-start.2 = (f32[2,3,2,64,128]{4,3,2,1,0:T(8,128)S(1)}, f32[2,3,2,64,128]{4,3,2,1,0:T(8,128)}, u32[]{:S(2)}) copy-start(f32[2,3,2,64,128]{4,3,2,1,0:T(8,128)} %disp_hbm.3) | copy-start | bytes 1179652
  0.7 5.1 %copy-start.1 = (f32[2,3,2,64,128]{4,3,2,1,0:T(8,128)S(1)}, f32[2,3,2,64,128]{4,3,2,1,0:T(8,128)}, u32[]{:S(2)}) copy-start(f32[2,3,2,64,128]{4,3,2,1,0:T(8,128)} %vel_hbm.3) | copy-start | bytes 1179652
  0.7 5.0 %copy-start.3 = (f32[2,2,64,128]{3,2,1,0:T(8,128)S(1)}, f32[2,2,64,128]{3,2,1,0:T(8,128)}, u32[]{:S(2)}) copy-start(f32[2,2,64,128]{3,2,1,0:T(8,128)} %init_hbm.3) | copy-start | bytes 393220
  2.9 7.4 %copy-start = (bf16[256,2,64,128]{3,2,1,0:T(8,128)(2,1)S(1)}, bf16[256,2,64,128]{3,2,1,0:T(8,128)(2,1)}, u32[]{:S(2)}) copy-start(bf16[256,2,64,128]{3,2,1,0:T(8,128)(2,1)} %held_ref.1) | copy-start | bytes 25165828
  2.9 7.3 %collective-permute-start.1 = (f32[8,64,128]{2,1,0:T(8,128)}, f32[8,64,128]{2,1,0:T(8,128)S(1)}, u32[]{:S(2)}, u32[]{:S(2)}) collective-permute-start(f32[8,64,128]{2,1,0:T(8,128)} %shard_map.85), channel_id=1, source_target_pairs={{0,64},{1,2},{2,1},{3,4},{4,3},{5,6},{6,5},{7,8},{8,7},{9,10},{10,... | collective-permute-start | bytes 786440 | tf_op jit(solution)/shard_map/ppermute | solution.py:339
  6.7 3.6 %collective-permute-start = (f32[8,64,128]{2,1,0:T(8,128)S(1)}, f32[8,64,128]{2,1,0:T(8,128)S(1)}, u32[]{:S(2)}, u32[]{:S(2)}) collective-permute-start(f32[8,64,128]{2,1,0:T(8,128)S(1)} %get-tuple-element.13), channel_id=1, source_target_pairs={{0,1},{1,0},{2,3},{3,2},{4,5},{5,4},{6,7},{7,6},{8,9},{9,8},{10,11... | collective-permute-start | bytes 786440 | tf_op jit(solution)/shard_map/ppermute | solution.py:340
  14.0 14.0 %all-to-all-start = ((f32[32,1,512]{2,1,0:T(1,128)}), f32[32,1,512]{2,1,0:T(1,128)S(1)}, u32[]{:S(2)}, u32[]{:S(2)}) async-start(f32[32,1,512]{2,1,0:T(1,128)} %broadcast_in_dim.16), calls=%async_computation | async-start | bytes 131072 | tf_op jit(solution)/shard_map/all_to_all | solution.py:353
  24.3 15.0 %collective-permute-start.4 = (f32[2,2,64,128]{3,2,1,0:T(8,128)S(1)}, f32[2,2,64,128]{3,2,1,0:T(8,128)S(1)}, u32[]{:S(2)}, u32[]{:S(2)}) collective-permute-start(f32[2,2,64,128]{3,2,1,0:T(8,128)S(1)} %get-tuple-element.15.refs_0_), channel_id=1, source_target_pairs={{0,192},{64,128},{128,64},{192,0},{1,193},{65,129},{129,65},{193,1... | collective-permute-start | bytes 393224 | tf_op jit(solution)/shard_map/ppermute | solution.py:361
  24.5 14.7 %collective-permute-start.3 = (f32[2,2,64,128]{3,2,1,0:T(8,128)S(1)}, f32[2,2,64,128]{3,2,1,0:T(8,128)S(1)}, u32[]{:S(2)}, u32[]{:S(2)}) collective-permute-start(f32[2,2,64,128]{3,2,1,0:T(8,128)S(1)} %get-tuple-element.15.refs_0_), channel_id=1, source_target_pairs={{0,128},{64,192},{128,0},{192,64},{1,129},{65,193},{129,1},{193,65... | collective-permute-start | bytes 393224 | tf_op jit(solution)/shard_map/ppermute | solution.py:361
  26.7 12.6 %collective-permute-start.2 = (f32[2,2,64,128]{3,2,1,0:T(8,128)S(1)}, f32[2,2,64,128]{3,2,1,0:T(8,128)S(1)}, u32[]{:S(2)}, u32[]{:S(2)}) collective-permute-start(f32[2,2,64,128]{3,2,1,0:T(8,128)S(1)} %get-tuple-element.15.refs_0_), channel_id=1, source_target_pairs={{0,64},{64,0},{128,192},{192,128},{1,65},{65,1},{129,193},{193,129... | collective-permute-start | bytes 393224 | tf_op jit(solution)/shard_map/ppermute | solution.py:361
  28.6 13.0 %all-to-all-start.1 = ((f32[8,1,2048]{2,1,0:T(1,128)}), f32[8,1,2048]{2,1,0:T(1,128)S(1)}, u32[]{:S(2)}, u32[]{:S(2)}) async-start(f32[8,1,2048]{2,1,0:T(1,128)} %broadcast_in_dim.18), calls=%async_computation.1 | async-start | bytes 131072 | tf_op jit(solution)/shard_map/all_to_all | solution.py:353

commit v5 on v4

--- a/solution.py
+++ b/solution.py
@@ -343,7 +343,7 @@
         step_kernel,
         (jax.ShapeDtypeStruct(initial.shape, f32), jax.ShapeDtypeStruct(line, f32)),
         [vmem] * 4,
-        [pltpu.VMEM((components * 8, count * rows), f32)],
+        [pltpu.VMEM((components * 8 + 8, count * rows), f32)],
     )(kept, near, far, basis)
 
     everything = np.arange(reals * cells).reshape(reals, deep, wide * cores)
@@ -352,7 +352,8 @@
         sent = jnp.broadcast_to(a[None], (groups.shape[1], *a.shape))
         return lax.all_to_all(sent, AXES, 0, 0, axis_index_groups=groups.tolist(), tiled=True)
 
-    parts = spread_out(coords, everything.transpose(1, 0, 2).reshape(deep, -1)[:, ::-1])
+    rolled = np.roll(everything, reals // 2 - 1, axis=0)
+    parts = spread_out(coords, rolled.transpose(1, 0, 2).reshape(deep, -1)[:, ::-1])
     coords = parts.reshape(reals, wide * cores, -1).sum(axis=1).reshape(1, -1)
     parts = spread_out(
         coords, np.roll(everything.transpose(0, 2, 1).reshape(-1, deep), deep // 2, axis=1)

time: 43.1 us -> 42.9 us (level)
  transfers between devices with their start and end apart: 7 -> 7, of which waited for: 3 -> 2; matrix products, arithmetic and copies ran while one was open for 2% -> 2% of each run, Pallas kernels for 2% -> 2%
where the time goes in v5:
time: 42.9 us; the launch traced here: 42.5 us
  starting transfers between devices  27.7 us (65%)
  Pallas kernels  7.39 us (17%)
  waiting for transfers between devices  5.33 us (12%)
  local copies, waits for them, and re-layouts  1.39 us (3%)
  between operations  0.72 us (2%)
    all_to_all x2, starting transfers between devices, spread_out(): lax.all_to_all(sent, AXES, 0, 0, axis_index_groups=groups.tolist(), tiled...  20.9 us
    ppermute x3, starting transfers between devices, shards(): lax.ppermute(conc, 'real', [(i, i ^ k) for i in range(reals)])  3.34 us
    pallas_call x1, Pallas kernels, shards(): call(step_kernel, (jax.ShapeDtypeStruct(initial.shape, f32), jax.ShapeDty...  2.99 us
    ppermute x1, waiting for transfers between devices, shards(): far = lax.ppermute(far, AXES, pairs)  2.92 us
    ppermute x1, starting transfers between devices, shards(): far = lax.ppermute(far, AXES, pairs)  2.77 us
    all_to_all x2, waiting for transfers between devices, spread_out(): lax.all_to_all(sent, AXES, 0, 0, axis_index_groups=groups.tolist(), tiled...  2.4 us
    pallas_call x1, Pallas kernels, shards(): call(pack_kernel, packed, [hbm] * 4, own + [pltpu.VMEM(packed.shape, f32)...  2.23 us
    broadcast_in_dim x2, local copies, waits for them, and re-layouts, spread_out(): sent = jnp.broadcast_to(a[None], (groups.shape[1], *a.shape))  1.36 us
  transfers between devices with their start and end apart: 7, of which 2 were waited for; matrix products, arithmetic and copies ran while one was open for 2% of the time, Pallas kernels for 2%

profile of v5, /device:TPU:1, one launch (start us, length us, event | category | flops | bytes accessed | tf_op | source)
XLA Modules:
  0.0 42.5 jit_solution(8651199672626522921)
XLA Ops:
  0.6 0.0 copy-start.4
  0.6 0.0 copy-start.2
  0.7 0.0 copy-start.1
  0.7 0.0 copy-start.3
  0.7 2.2 %shard_map.85 = f32[8,64,128]{2,1,0:T(8,128)} custom-call(f32[2,2,64,128]{3,2,1,0:T(8,128)} %init_hbm.3, f32[2,3,2,64,128]{4,3,2,1,0:T(8,128)} %vel_hbm.3, f32[2,3,2,64,128]{4,3,2,1,0:T(8,128)} %disp_hbm.3, s32[2,64]{1,0:T(2,128)} %bounds_hbm.3), custom_call_target="tpu_custom_call" | custom-call | flops 10000000000 | bytes 30000000 | tf_op jit(solution)/shard_map/pallas_call | solution.py:314
  2.9 0.0 copy-start
  2.9 2.8 %collective-permute-start.1 = (f32[8,64,128]{2,1,0:T(8,128)}, f32[8,64,128]{2,1,0:T(8,128)S(1)}, u32[]{:S(2)}, u32[]{:S(2)}) collective-permute-start(f32[8,64,128]{2,1,0:T(8,128)} %shard_map.85), channel_id=1, source_target_pairs={{0,64},{1,2},{2,1},{3,4},{4,3},{5,6},{6,5},{7,8},{8,7},{9,10},{10,... | collective-permute-start | bytes 786440 | tf_op jit(solution)/shard_map/ppermute | solution.py:339
  5.7 0.0 copy-done.4
  5.7 0.0 copy-done.2
  5.7 0.0 copy-done.1
  5.7 0.0 copy-done.3
  5.7 0.9 %shard_map.84 = (f32[8,64,128]{2,1,0:T(8,128)S(1)}, f32[2,18,64,128]{3,2,1,0:T(8,128)S(1)}) custom-call(f32[2,2,64,128]{3,2,1,0:T(8,128)S(1)} %copy-done.3, f32[2,3,2,64,128]{4,3,2,1,0:T(8,128)S(1)} %copy-done.1, f32[2,3,2,64,128]{4,3,2,1,0:T(8,128)S(1)} %copy-done.2, s32[2,64]{1,0:T(2,128)S(1)} %copy-done.4), custom_call_target="tpu_custom_call" | custom-call | flops 10000000000 | bytes 30000000 | tf_op jit(solution)/shard_map/pallas_call | solution.py:325
  6.7 0.7 %collective-permute-start = (f32[8,64,128]{2,1,0:T(8,128)S(1)}, f32[8,64,128]{2,1,0:T(8,128)S(1)}, u32[]{:S(2)}, u32[]{:S(2)}) collective-permute-start(f32[8,64,128]{2,1,0:T(8,128)S(1)} %get-tuple-element.13), channel_id=1, source_target_pairs={{0,1},{1,0},{2,3},{3,2},{4,5},{5,4},{6,7},{7,6},{8,9},{9,8},{10,11... | collective-permute-start | bytes 786440 | tf_op jit(solution)/shard_map/ppermute | solution.py:340
  7.3 2.9 %collective-permute-done.1.far_ref = f32[8,64,128]{2,1,0:T(8,128)S(1)} collective-permute-done((f32[8,64,128]{2,1,0:T(8,128)}, f32[8,64,128]{2,1,0:T(8,128)S(1)}, u32[]{:S(2)}, u32[]{:S(2)}) %collective-permute-start.1) | collective-permute-done | bytes 262176 | tf_op jit(solution)/shard_map/ppermute | solution.py:339
  10.3 0.0 collective-permute-done.near_ref
  10.3 0.0 copy-done
  10.3 3.0 %shard_map.86 = (f32[2,2,64,128]{3,2,1,0:T(8,128)S(1)}, f32[1,512]{1,0:T(1,128)S(1)}) custom-call(f32[2,18,64,128]{3,2,1,0:T(8,128)S(1)} %get-tuple-element.12.kept_ref, f32[8,64,128]{2,1,0:T(8,128)S(1)} %collective-permute-done.near_ref, f32[8,64,128]{2,1,0:T(8,128)S(1)} %collective-permute-done.1.far_ref, bf16[256,2,64,128]{3,2,1,0:T(8,128)(2,1)S(1)} %copy-done), custom_call_target="tpu_custom_call" | custom-call | tf_op jit(solution)/shard_map/pallas_call | solution.py:342
  13.3 0.7 %broadcast_in_dim.16 = f32[32,1,512]{2,1,0:T(1,128)} broadcast(f32[512]{0:T(512)S(1)} %bitcast.6), dimensions={2} | broadcast | bytes 67584 | tf_op jit(solution)/shard_map/broadcast_in_dim | solution.py:352
  14.0 10.5 %all-to-all-start = ((f32[32,1,512]{2,1,0:T(1,128)}), f32[32,1,512]{2,1,0:T(1,128)S(1)}, u32[]{:S(2)}, u32[]{:S(2)}) async-start(f32[32,1,512]{2,1,0:T(1,128)} %broadcast_in_dim.16), calls=%async_computation | async-start | bytes 131072 | tf_op jit(solution)/shard_map/all_to_all | solution.py:353
  24.5 0.4 collective-permute-start.4
  24.9 1.1 %collective-permute-start.3 = (f32[2,2,64,128]{3,2,1,0:T(8,128)S(1)}, f32[2,2,64,128]{3,2,1,0:T(8,128)S(1)}, u32[]{:S(2)}, u32[]{:S(2)}) collective-permute-start(f32[2,2,64,128]{3,2,1,0:T(8,128)S(1)} %get-tuple-element.15.refs_0_), channel_id=1, source_target_pairs={{0,128},{64,192},{128,0},{192,64},{1,129},{65,193},{129,1},{193,65... | collective-permute-start | bytes 393224 | tf_op jit(solution)/shard_map/ppermute | solution.py:362
  26.0 1.8 %collective-permute-start.2 = (f32[2,2,64,128]{3,2,1,0:T(8,128)S(1)}, f32[2,2,64,128]{3,2,1,0:T(8,128)S(1)}, u32[]{:S(2)}, u32[]{:S(2)}) collective-permute-start(f32[2,2,64,128]{3,2,1,0:T(8,128)S(1)} %get-tuple-element.15.refs_0_), channel_id=1, source_target_pairs={{0,64},{64,0},{128,192},{192,128},{1,65},{65,1},{129,193},{193,129... | collective-permute-start | bytes 393224 | tf_op jit(solution)/shard_map/ppermute | solution.py:362
  27.9 0.0 all-to-all-done
  27.9 0.7 %broadcast_in_dim.18 = f32[8,1,2048]{2,1,0:T(1,128)} broadcast(f32[2048]{0:T(1024)S(1)} %bitcast.8), dimensions={2} | broadcast | bytes 73728 | tf_op jit(solution)/shard_map/broadcast_in_dim | solution.py:352
  28.6 10.3 %all-to-all-start.1 = ((f32[8,1,2048]{2,1,0:T(1,128)}), f32[8,1,2048]{2,1,0:T(1,128)S(1)}, u32[]{:S(2)}, u32[]{:S(2)}) async-start(f32[8,1,2048]{2,1,0:T(1,128)} %broadcast_in_dim.18), calls=%async_computation.1 | async-start | bytes 131072 | tf_op jit(solution)/shard_map/all_to_all | solution.py:353
  38.9 0.0 collective-permute-done.4.refs_3_
  38.9 0.0 collective-permute-done.3.refs_2_
  38.9 0.0 collective-permute-done.2.refs_1_
  38.9 2.4 %all-to-all-done.1.parts_ref = f32[8,1,2048]{2,1,0:T(1,128)S(1)} async-done(((f32[8,1,2048]{2,1,0:T(1,128)}), f32[8,1,2048]{2,1,0:T(1,128)S(1)}, u32[]{:S(2)}, u32[]{:S(2)}) %all-to-all-start.1) | async-done | bytes 65568 | tf_op jit(solution)/shard_map/all_to_all | solution.py:353
  41.3 1.2 %shard_map.87 = (f32[2,64,128]{2,1,0:T(8,128)}, f32[2,64,128]{2,1,0:T(8,128)}, f32[1,256]{1,0:T(1,128)}, f32[256,256]{1,0:T(8,128)}) custom-call(f32[8,1,2048]{2,1,0:T(1,128)S(1)} %all-to-all-done.1.parts_ref, f32[2,2,64,128]{3,2,1,0:T(8,128)S(1)} %get-tuple-element.15.refs_0_, f32[2,2,64,128]{3,2,1,0:T(8,128)S(1)} %collective-permute-done.2.refs_1_, ...), custom_call_target="tpu_custom_call" | custom-call | tf_op jit(solution)/shard_map/pallas_call | solution.py:365
  (2 shorter events, 0.0 us)
Async XLA Ops:
  0.6 5.1 %copy-start.4 = (s32[2,64]{1,0:T(2,128)S(1)}, s32[2,64]{1,0:T(2,128)}, u32[]{:S(2)}) copy-start(s32[2,64]{1,0:T(2,128)} %bounds_hbm.3) | copy-start | bytes 1540
  0.6 5.1 %copy-start.2 = (f32[2,3,2,64,128]{4,3,2,1,0:T(8,128)S(1)}, f32[2,3,2,64,128]{4,3,2,1,0:T(8,128)}, u32[]{:S(2)}) copy-start(f32[2,3,2,64,128]{4,3,2,1,0:T(8,128)} %disp_hbm.3) | copy-start | bytes 1179652
  0.7 5.1 %copy-start.1 = (f32[2,3,2,64,128]{4,3,2,1,0:T(8,128)S(1)}, f32[2,3,2,64,128]{4,3,2,1,0:T(8,128)}, u32[]{:S(2)}) copy-start(f32[2,3,2,64,128]{4,3,2,1,0:T(8,128)} %vel_hbm.3) | copy-start | bytes 1179652
  0.7 5.0 %copy-start.3 = (f32[2,2,64,128]{3,2,1,0:T(8,128)S(1)}, f32[2,2,64,128]{3,2,1,0:T(8,128)}, u32[]{:S(2)}) copy-start(f32[2,2,64,128]{3,2,1,0:T(8,128)} %init_hbm.3) | copy-start | bytes 393220
  2.9 7.4 %copy-start = (bf16[256,2,64,128]{3,2,1,0:T(8,128)(2,1)S(1)}, bf16[256,2,64,128]{3,2,1,0:T(8,128)(2,1)}, u32[]{:S(2)}) copy-start(bf16[256,2,64,128]{3,2,1,0:T(8,128)(2,1)} %held_ref.1) | copy-start | bytes 25165828
  2.9 7.3 %collective-permute-start.1 = (f32[8,64,128]{2,1,0:T(8,128)}, f32[8,64,128]{2,1,0:T(8,128)S(1)}, u32[]{:S(2)}, u32[]{:S(2)}) collective-permute-start(f32[8,64,128]{2,1,0:T(8,128)} %shard_map.85), channel_id=1, source_target_pairs={{0,64},{1,2},{2,1},{3,4},{4,3},{5,6},{6,5},{7,8},{8,7},{9,10},{10,... | collective-permute-start | bytes 786440 | tf_op jit(solution)/shard_map/ppermute | solution.py:339
  6.7 3.6 %collective-permute-start = (f32[8,64,128]{2,1,0:T(8,128)S(1)}, f32[8,64,128]{2,1,0:T(8,128)S(1)}, u32[]{:S(2)}, u32[]{:S(2)}) collective-permute-start(f32[8,64,128]{2,1,0:T(8,128)S(1)} %get-tuple-element.13), channel_id=1, source_target_pairs={{0,1},{1,0},{2,3},{3,2},{4,5},{5,4},{6,7},{7,6},{8,9},{9,8},{10,11... | collective-permute-start | bytes 786440 | tf_op jit(solution)/shard_map/ppermute | solution.py:340
  14.0 13.9 %all-to-all-start = ((f32[32,1,512]{2,1,0:T(1,128)}), f32[32,1,512]{2,1,0:T(1,128)S(1)}, u32[]{:S(2)}, u32[]{:S(2)}) async-start(f32[32,1,512]{2,1,0:T(1,128)} %broadcast_in_dim.16), calls=%async_computation | async-start | bytes 131072 | tf_op jit(solution)/shard_map/all_to_all | solution.py:353
  24.5 14.4 %collective-permute-start.4 = (f32[2,2,64,128]{3,2,1,0:T(8,128)S(1)}, f32[2,2,64,128]{3,2,1,0:T(8,128)S(1)}, u32[]{:S(2)}, u32[]{:S(2)}) collective-permute-start(f32[2,2,64,128]{3,2,1,0:T(8,128)S(1)} %get-tuple-element.15.refs_0_), channel_id=1, source_target_pairs={{0,192},{64,128},{128,64},{192,0},{1,193},{65,129},{129,65},{193,1... | collective-permute-start | bytes 393224 | tf_op jit(solution)/shard_map/ppermute | solution.py:362
  24.9 14.0 %collective-permute-start.3 = (f32[2,2,64,128]{3,2,1,0:T(8,128)S(1)}, f32[2,2,64,128]{3,2,1,0:T(8,128)S(1)}, u32[]{:S(2)}, u32[]{:S(2)}) collective-permute-start(f32[2,2,64,128]{3,2,1,0:T(8,128)S(1)} %get-tuple-element.15.refs_0_), channel_id=1, source_target_pairs={{0,128},{64,192},{128,0},{192,64},{1,129},{65,193},{129,1},{193,65... | collective-permute-start | bytes 393224 | tf_op jit(solution)/shard_map/ppermute | solution.py:362
  26.0 12.9 %collective-permute-start.2 = (f32[2,2,64,128]{3,2,1,0:T(8,128)S(1)}, f32[2,2,64,128]{3,2,1,0:T(8,128)S(1)}, u32[]{:S(2)}, u32[]{:S(2)}) collective-permute-start(f32[2,2,64,128]{3,2,1,0:T(8,128)S(1)} %get-tuple-element.15.refs_0_), channel_id=1, source_target_pairs={{0,64},{64,0},{128,192},{192,128},{1,65},{65,1},{129,193},{193,129... | collective-permute-start | bytes 393224 | tf_op jit(solution)/shard_map/ppermute | solution.py:362
  28.6 12.8 %all-to-all-start.1 = ((f32[8,1,2048]{2,1,0:T(1,128)}), f32[8,1,2048]{2,1,0:T(1,128)S(1)}, u32[]{:S(2)}, u32[]{:S(2)}) async-start(f32[8,1,2048]{2,1,0:T(1,128)} %broadcast_in_dim.18), calls=%async_computation.1 | async-start | bytes 131072 | tf_op jit(solution)/shard_map/all_to_all | solution.py:353

commit v6 on v5

--- a/solution.py
+++ b/solution.py
@@ -236,7 +236,9 @@
         preferred_element_type=jnp.float32,
     )
     for r in range(count):
-        coords_ref[:, r * components : (r + 1) * components] = coords[r : r + 1]
+        coords_ref[:, :, r * components : (r + 1) * components] = jnp.broadcast_to(
+            coords[r : r + 1][None], (coords_ref.shape[0], 1, components)
+        )
 
 
 def tree_sum(terms):
@@ -338,7 +340,7 @@
     ]
     far = lax.ppermute(far, AXES, pairs)
     near = lax.ppermute(near, "core", [(0, 1), (1, 0)])
-    line = (1, count * components)
+    line = (reals * wide * cores, 1, count * components)
     conc, coords = call(
         step_kernel,
         (jax.ShapeDtypeStruct(initial.shape, f32), jax.ShapeDtypeStruct(line, f32)),
@@ -349,12 +351,12 @@
     everything = np.arange(reals * cells).reshape(reals, deep, wide * cores)
 
     def spread_out(a, groups):
-        sent = jnp.broadcast_to(a[None], (groups.shape[1], *a.shape))
-        return lax.all_to_all(sent, AXES, 0, 0, axis_index_groups=groups.tolist(), tiled=True)
+        return lax.all_to_all(a, AXES, 0, 0, axis_index_groups=groups.tolist(), tiled=True)
 
     rolled = np.roll(everything, reals // 2 - 1, axis=0)
     parts = spread_out(coords, rolled.transpose(1, 0, 2).reshape(deep, -1)[:, ::-1])
     coords = parts.reshape(reals, wide * cores, -1).sum(axis=1).reshape(1, -1)
+    coords = jnp.broadcast_to(coords[None], (deep, *coords.shape))
     parts = spread_out(
         coords, np.roll(everything.transpose(0, 2, 1).reshape(-1, deep), deep // 2, axis=1)
     )

time: 42.9 us -> 42.9 us (level)
  local copies, waits for them, and re-layouts: 1.39 us -> 0.69 us
  Pallas kernels: 7.39 us -> 8.07 us
    broadcast_in_dim x2 -> x1, local copies, waits for them, and re-layouts: 1.36 us -> 0.66 us  [shards(): coords = jnp.broadcast_to(coords[None], (deep, *coords.shape))]
    pallas_call x1, Pallas kernels: 2.99 us -> 3.67 us  [shards(): call(step_kernel, (jax.ShapeDtypeStruct(initial.shape, f32), jax.ShapeDty...]
where the time goes in v6:
time: 42.9 us; the launch traced here: 42.5 us
  starting transfers between devices  27.7 us (65%)
  Pallas kernels  8.07 us (19%)
  waiting for transfers between devices  5.33 us (12%)
  between operations  0.72 us (2%)
  local copies, waits for them, and re-layouts  0.69 us (2%)
    all_to_all x2, starting transfers between devices, spread_out(): lax.all_to_all(a, AXES, 0, 0, axis_index_groups=groups.tolist(), tiled=True)  20.9 us
    pallas_call x1, Pallas kernels, shards(): call(step_kernel, (jax.ShapeDtypeStruct(initial.shape, f32), jax.ShapeDty...  3.67 us
    ppermute x3, starting transfers between devices, shards(): lax.ppermute(conc, 'real', [(i, i ^ k) for i in range(reals)])  3.34 us
    ppermute x1, waiting for transfers between devices, shards(): far = lax.ppermute(far, AXES, pairs)  2.92 us
    ppermute x1, starting transfers between devices, shards(): far = lax.ppermute(far, AXES, pairs)  2.77 us
    all_to_all x2, waiting for transfers between devices, spread_out(): lax.all_to_all(a, AXES, 0, 0, axis_index_groups=groups.tolist(), tiled=True)  2.4 us
    pallas_call x1, Pallas kernels, shards(): call(pack_kernel, packed, [hbm] * 4, own + [pltpu.VMEM(packed.shape, f32)...  2.23 us
    pallas_call x1, Pallas kernels, shards(): call(stats_kernel, tuple((jax.ShapeDtypeStruct(a, f32) for a in shapes)),...  1.24 us
  transfers between devices with their start and end apart: 7, of which 2 were waited for; matrix products, arithmetic and copies ran while one was open for 2% of the time, Pallas kernels for 2%

profile of v6, /device:TPU:1, one launch (start us, length us, event | category | flops | bytes accessed | tf_op | source)
XLA Modules:
  0.0 42.5 jit_solution(11636227859914787913)
XLA Ops:
  0.6 0.0 copy-start.4
  0.6 0.0 copy-start.2
  0.7 0.0 copy-start.1
  0.7 0.0 copy-start.3
  0.7 2.2 %shard_map.85 = f32[8,64,128]{2,1,0:T(8,128)} custom-call(f32[2,2,64,128]{3,2,1,0:T(8,128)} %init_hbm.3, f32[2,3,2,64,128]{4,3,2,1,0:T(8,128)} %vel_hbm.3, f32[2,3,2,64,128]{4,3,2,1,0:T(8,128)} %disp_hbm.3, s32[2,64]{1,0:T(2,128)} %bounds_hbm.3), custom_call_target="tpu_custom_call" | custom-call | flops 10000000000 | bytes 30000000 | tf_op jit(solution)/shard_map/pallas_call | solution.py:316
  2.9 0.0 copy-start
  2.9 2.8 %collective-permute-start.1 = (f32[8,64,128]{2,1,0:T(8,128)}, f32[8,64,128]{2,1,0:T(8,128)S(1)}, u32[]{:S(2)}, u32[]{:S(2)}) collective-permute-start(f32[8,64,128]{2,1,0:T(8,128)} %shard_map.85), channel_id=1, source_target_pairs={{0,64},{1,2},{2,1},{3,4},{4,3},{5,6},{6,5},{7,8},{8,7},{9,10},{10,... | collective-permute-start | bytes 786440 | tf_op jit(solution)/shard_map/ppermute | solution.py:341
  5.7 0.0 copy-done.4
  5.7 0.0 copy-done.2
  5.7 0.0 copy-done.1
  5.7 0.0 copy-done.3
  5.7 0.9 %shard_map.84 = (f32[8,64,128]{2,1,0:T(8,128)S(1)}, f32[2,18,64,128]{3,2,1,0:T(8,128)S(1)}) custom-call(f32[2,2,64,128]{3,2,1,0:T(8,128)S(1)} %copy-done.3, f32[2,3,2,64,128]{4,3,2,1,0:T(8,128)S(1)} %copy-done.1, f32[2,3,2,64,128]{4,3,2,1,0:T(8,128)S(1)} %copy-done.2, s32[2,64]{1,0:T(2,128)S(1)} %copy-done.4), custom_call_target="tpu_custom_call" | custom-call | flops 10000000000 | bytes 30000000 | tf_op jit(solution)/shard_map/pallas_call | solution.py:327
  6.7 0.7 %collective-permute-start = (f32[8,64,128]{2,1,0:T(8,128)S(1)}, f32[8,64,128]{2,1,0:T(8,128)S(1)}, u32[]{:S(2)}, u32[]{:S(2)}) collective-permute-start(f32[8,64,128]{2,1,0:T(8,128)S(1)} %get-tuple-element.13), channel_id=1, source_target_pairs={{0,1},{1,0},{2,3},{3,2},{4,5},{5,4},{6,7},{7,6},{8,9},{9,8},{10,11... | collective-permute-start | bytes 786440 | tf_op jit(solution)/shard_map/ppermute | solution.py:342
  7.3 2.9 %collective-permute-done.1.far_ref = f32[8,64,128]{2,1,0:T(8,128)S(1)} collective-permute-done((f32[8,64,128]{2,1,0:T(8,128)}, f32[8,64,128]{2,1,0:T(8,128)S(1)}, u32[]{:S(2)}, u32[]{:S(2)}) %collective-permute-start.1) | collective-permute-done | bytes 262176 | tf_op jit(solution)/shard_map/ppermute | solution.py:341
  10.3 0.0 collective-permute-done.near_ref
  10.3 0.0 copy-done
  10.3 3.7 %shard_map.86 = (f32[2,2,64,128]{3,2,1,0:T(8,128)S(1)}, f32[32,1,512]{2,1,0:T(1,128)}) custom-call(f32[2,18,64,128]{3,2,1,0:T(8,128)S(1)} %get-tuple-element.12.kept_ref, f32[8,64,128]{2,1,0:T(8,128)S(1)} %collective-permute-done.near_ref, f32[8,64,128]{2,1,0:T(8,128)S(1)} %collective-permute-done.1.far_ref, bf16[256,2,64,128]{3,2,1,0:T(8,128)(2,1)S(1)} %copy-done), custom_call_target="tpu_custom_call" | custom-call | tf_op jit(solution)/shard_map/pallas_call | solution.py:344
  13.9 10.5 %all-to-all-start = ((f32[32,1,512]{2,1,0:T(1,128)}), f32[32,1,512]{2,1,0:T(1,128)S(1)}, u32[]{:S(2)}, u32[]{:S(2)}) async-start(f32[32,1,512]{2,1,0:T(1,128)} %get-tuple-element.14), calls=%async_computation | async-start | bytes 131072 | tf_op jit(solution)/shard_map/all_to_all | solution.py:354
  24.5 0.4 collective-permute-start.4
  24.9 1.1 %collective-permute-start.3 = (f32[2,2,64,128]{3,2,1,0:T(8,128)S(1)}, f32[2,2,64,128]{3,2,1,0:T(8,128)S(1)}, u32[]{:S(2)}, u32[]{:S(2)}) collective-permute-start(f32[2,2,64,128]{3,2,1,0:T(8,128)S(1)} %get-tuple-element.15.refs_0_), channel_id=1, source_target_pairs={{0,128},{64,192},{128,0},{192,64},{1,129},{65,193},{129,1},{193,65... | collective-permute-start | bytes 393224 | tf_op jit(solution)/shard_map/ppermute | solution.py:364
  26.0 1.8 %collective-permute-start.2 = (f32[2,2,64,128]{3,2,1,0:T(8,128)S(1)}, f32[2,2,64,128]{3,2,1,0:T(8,128)S(1)}, u32[]{:S(2)}, u32[]{:S(2)}) collective-permute-start(f32[2,2,64,128]{3,2,1,0:T(8,128)S(1)} %get-tuple-element.15.refs_0_), channel_id=1, source_target_pairs={{0,64},{64,0},{128,192},{192,128},{1,65},{65,1},{129,193},{193,129... | collective-permute-start | bytes 393224 | tf_op jit(solution)/shard_map/ppermute | solution.py:364
  27.8 0.0 all-to-all-done
  27.9 0.7 %broadcast_in_dim.8 = f32[8,1,2048]{2,1,0:T(1,128)} broadcast(f32[2048]{0:T(1024)S(1)} %bitcast.6), dimensions={2} | broadcast | bytes 73728 | tf_op jit(solution)/shard_map/broadcast_in_dim | solution.py:359
  28.5 10.3 %all-to-all-start.1 = ((f32[8,1,2048]{2,1,0:T(1,128)}), f32[8,1,2048]{2,1,0:T(1,128)S(1)}, u32[]{:S(2)}, u32[]{:S(2)}) async-start(f32[8,1,2048]{2,1,0:T(1,128)} %broadcast_in_dim.8), calls=%async_computation.1 | async-start | bytes 131072 | tf_op jit(solution)/shard_map/all_to_all | solution.py:354
  38.9 0.0 collective-permute-done.4.refs_3_
  38.9 0.0 collective-permute-done.3.refs_2_
  38.9 0.0 collective-permute-done.2.refs_1_
  38.9 2.4 %all-to-all-done.1.parts_ref = f32[8,1,2048]{2,1,0:T(1,128)S(1)} async-done(((f32[8,1,2048]{2,1,0:T(1,128)}), f32[8,1,2048]{2,1,0:T(1,128)S(1)}, u32[]{:S(2)}, u32[]{:S(2)}) %all-to-all-start.1) | async-done | bytes 65568 | tf_op jit(solution)/shard_map/all_to_all | solution.py:354
  41.3 1.2 %shard_map.87 = (f32[2,64,128]{2,1,0:T(8,128)}, f32[2,64,128]{2,1,0:T(8,128)}, f32[1,256]{1,0:T(1,128)}, f32[256,256]{1,0:T(8,128)}) custom-call(f32[8,1,2048]{2,1,0:T(1,128)S(1)} %all-to-all-done.1.parts_ref, f32[2,2,64,128]{3,2,1,0:T(8,128)S(1)} %get-tuple-element.15.refs_0_, f32[2,2,64,128]{3,2,1,0:T(8,128)S(1)} %collective-permute-done.2.refs_1_, ...), custom_call_target="tpu_custom_call" | custom-call | tf_op jit(solution)/shard_map/pallas_call | solution.py:367
  (2 shorter events, 0.0 us)
Async XLA Ops:
  0.6 5.1 %copy-start.4 = (s32[2,64]{1,0:T(2,128)S(1)}, s32[2,64]{1,0:T(2,128)}, u32[]{:S(2)}) copy-start(s32[2,64]{1,0:T(2,128)} %bounds_hbm.3) | copy-start | bytes 1540
  0.6 5.1 %copy-start.2 = (f32[2,3,2,64,128]{4,3,2,1,0:T(8,128)S(1)}, f32[2,3,2,64,128]{4,3,2,1,0:T(8,128)}, u32[]{:S(2)}) copy-start(f32[2,3,2,64,128]{4,3,2,1,0:T(8,128)} %disp_hbm.3) | copy-start | bytes 1179652
  0.7 5.1 %copy-start.1 = (f32[2,3,2,64,128]{4,3,2,1,0:T(8,128)S(1)}, f32[2,3,2,64,128]{4,3,2,1,0:T(8,128)}, u32[]{:S(2)}) copy-start(f32[2,3,2,64,128]{4,3,2,1,0:T(8,128)} %vel_hbm.3) | copy-start | bytes 1179652
  0.7 5.0 %copy-start.3 = (f32[2,2,64,128]{3,2,1,0:T(8,128)S(1)}, f32[2,2,64,128]{3,2,1,0:T(8,128)}, u32[]{:S(2)}) copy-start(f32[2,2,64,128]{3,2,1,0:T(8,128)} %init_hbm.3) | copy-start | bytes 393220
  2.9 7.4 %copy-start = (bf16[256,2,64,128]{3,2,1,0:T(8,128)(2,1)S(1)}, bf16[256,2,64,128]{3,2,1,0:T(8,128)(2,1)}, u32[]{:S(2)}) copy-start(bf16[256,2,64,128]{3,2,1,0:T(8,128)(2,1)} %held_ref.1) | copy-start | bytes 25165828
  2.9 7.3 %collective-permute-start.1 = (f32[8,64,128]{2,1,0:T(8,128)}, f32[8,64,128]{2,1,0:T(8,128)S(1)}, u32[]{:S(2)}, u32[]{:S(2)}) collective-permute-start(f32[8,64,128]{2,1,0:T(8,128)} %shard_map.85), channel_id=1, source_target_pairs={{0,64},{1,2},{2,1},{3,4},{4,3},{5,6},{6,5},{7,8},{8,7},{9,10},{10,... | collective-permute-start | bytes 786440 | tf_op jit(solution)/shard_map/ppermute | solution.py:341
  6.7 3.6 %collective-permute-start = (f32[8,64,128]{2,1,0:T(8,128)S(1)}, f32[8,64,128]{2,1,0:T(8,128)S(1)}, u32[]{:S(2)}, u32[]{:S(2)}) collective-permute-start(f32[8,64,128]{2,1,0:T(8,128)S(1)} %get-tuple-element.13), channel_id=1, source_target_pairs={{0,1},{1,0},{2,3},{3,2},{4,5},{5,4},{6,7},{7,6},{8,9},{9,8},{10,11... | collective-permute-start | bytes 786440 | tf_op jit(solution)/shard_map/ppermute | solution.py:342
  13.9 13.9 %all-to-all-start = ((f32[32,1,512]{2,1,0:T(1,128)}), f32[32,1,512]{2,1,0:T(1,128)S(1)}, u32[]{:S(2)}, u32[]{:S(2)}) async-start(f32[32,1,512]{2,1,0:T(1,128)} %get-tuple-element.14), calls=%async_computation | async-start | bytes 131072 | tf_op jit(solution)/shard_map/all_to_all | solution.py:354
  24.5 14.4 %collective-permute-start.4 = (f32[2,2,64,128]{3,2,1,0:T(8,128)S(1)}, f32[2,2,64,128]{3,2,1,0:T(8,128)S(1)}, u32[]{:S(2)}, u32[]{:S(2)}) collective-permute-start(f32[2,2,64,128]{3,2,1,0:T(8,128)S(1)} %get-tuple-element.15.refs_0_), channel_id=1, source_target_pairs={{0,192},{64,128},{128,64},{192,0},{1,193},{65,129},{129,65},{193,1... | collective-permute-start | bytes 393224 | tf_op jit(solution)/shard_map/ppermute | solution.py:364
  24.9 14.0 %collective-permute-start.3 = (f32[2,2,64,128]{3,2,1,0:T(8,128)S(1)}, f32[2,2,64,128]{3,2,1,0:T(8,128)S(1)}, u32[]{:S(2)}, u32[]{:S(2)}) collective-permute-start(f32[2,2,64,128]{3,2,1,0:T(8,128)S(1)} %get-tuple-element.15.refs_0_), channel_id=1, source_target_pairs={{0,128},{64,192},{128,0},{192,64},{1,129},{65,193},{129,1},{193,65... | collective-permute-start | bytes 393224 | tf_op jit(solution)/shard_map/ppermute | solution.py:364
  26.0 12.9 %collective-permute-start.2 = (f32[2,2,64,128]{3,2,1,0:T(8,128)S(1)}, f32[2,2,64,128]{3,2,1,0:T(8,128)S(1)}, u32[]{:S(2)}, u32[]{:S(2)}) collective-permute-start(f32[2,2,64,128]{3,2,1,0:T(8,128)S(1)} %get-tuple-element.15.refs_0_), channel_id=1, source_target_pairs={{0,64},{64,0},{128,192},{192,128},{1,65},{65,1},{129,193},{193,129... | collective-permute-start | bytes 393224 | tf_op jit(solution)/shard_map/ppermute | solution.py:364
  28.5 12.8 %all-to-all-start.1 = ((f32[8,1,2048]{2,1,0:T(1,128)}), f32[8,1,2048]{2,1,0:T(1,128)S(1)}, u32[]{:S(2)}, u32[]{:S(2)}) async-start(f32[8,1,2048]{2,1,0:T(1,128)} %broadcast_in_dim.8), calls=%async_computation.1 | async-start | bytes 131072 | tf_op jit(solution)/shard_map/all_to_all | solution.py:354
